TPU v7x, 32 devices: a whole 2x2x4 slice. The times are simulated.
32 devices in a mesh: dp: 4 (over x, core), mp: 8 (over z, y).
Axes of the slice: x: 2, y: 2, z: 4, core: 2. Of those that a mesh axis runs over, the one named last changes fastest.
Arguments:
- acts: bfloat16 [512, 8192], P('dp', 'mp'), may hold values from -6 to 6
- grad_out: bfloat16 [512, 7168], P('dp', 'mp'), may hold values from -6 to 6
- values: bfloat16 [56, 20, 128, 128], P('mp', None, 'dp'), may hold values from -0.125 to 0.125
- block_rows: int32 [56, 20], P('mp'), may hold values from 0 to 63, as said below
- block_count: int32 [56], P('mp'), may hold values from 12 to 20, as said below
Outputs:
- hidden_out: bfloat16 [512, 7168], P('dp', 'mp')
- grad_acts: bfloat16 [512, 8192], P('dp', 'mp')
- grad_values: float32 [56, 20, 128, 128], P('mp', None, 'dp')
Inputs may be any that keep to these rules, and one draw needn't show every extreme that they name: `block_rows`: the live slots of a block column name distinct block rows; the first ones follow a butterfly pattern around block row c % 64. Slots at or after block_count are ignored. `block_count`: some block column has all 20 slots live.
All inputs are finite; a program needn't handle non-finite values.
Results may differ from a plain program's by a relative error of at most 0.02.
Values may be sent and summed in bfloat16 or wider, within the bound.
A program may use at most 128 MiB of HBM per device.

v0:
```python
import jax
import jax.numpy as jnp
from jax import lax
from jax.sharding import PartitionSpec as P


def shards(acts, grad_out, values, block_rows, block_count):
    tok_rows = acts.shape[0]
    col_blocks = values.shape[0]
    slot_count = values.shape[1]
    block_size = values.shape[3]
    whole = lax.all_gather(acts, "mp", axis=1, tiled=True)
    row_blocks = whole.shape[1] // block_size
    blocked = whole.reshape(tok_rows, row_blocks, block_size)
    weights_all = lax.all_gather(values, "dp", axis=2, tiled=True)
    slot_live = jnp.arange(slot_count, dtype=jnp.int32)[None, :] < block_count[:, None]
    masked = jnp.where(slot_live[:, :, None, None], weights_all, jnp.zeros((), jnp.bfloat16))
    grad_blocks = grad_out.reshape(tok_rows, col_blocks, block_size)
    outputs = []
    local_grads = []
    partial_value = jnp.zeros((tok_rows, row_blocks, block_size), jnp.float32)
    for column in range(col_blocks):
        picked = jnp.take(blocked, block_rows[column], axis=1)
        upstream = grad_blocks[:, column]
        outputs.append(
            jnp.einsum("tki,kij->tj", picked, masked[column], preferred_element_type=jnp.float32)
        )
        contrib = jnp.einsum(
            "tj,kij->tki", upstream, masked[column], preferred_element_type=jnp.float32
        )
        partial_value = partial_value.at[:, block_rows[column]].add(contrib)
        local_grads.append(
            jnp.einsum("tki,tj->kij", picked, upstream, preferred_element_type=jnp.float32)
        )
    hidden_out = jnp.concatenate(outputs, axis=1).astype(jnp.bfloat16)
    rounded_partial = partial_value.reshape(tok_rows, row_blocks * block_size).astype(jnp.bfloat16)
    grad_acts = (
        lax.psum_scatter(rounded_partial, "mp", scatter_dimension=1, tiled=True)
        .astype(jnp.float32)
        .astype(jnp.bfloat16)
    )
    stacked = jnp.stack(local_grads)
    stacked = jnp.where(slot_live[:, :, None, None], stacked, jnp.zeros((), jnp.float32))
    grad_values = lax.psum_scatter(
        stacked.astype(jnp.bfloat16), "dp", scatter_dimension=2, tiled=True
    ).astype(jnp.float32)
    return (hidden_out, grad_acts, grad_values)


def solution(mesh):
    placed = (P("dp", "mp"), P("dp", "mp"), P("mp", None, "dp", None), P("mp", None), P("mp"))
    return jax.shard_map(
        shards,
        mesh=mesh,
        in_specs=placed,
        out_specs=(P("dp", "mp"), P("dp", "mp"), P("mp", None, "dp", None)),
        check_vma=False,
    )
```

profile of v0, /device:TPU:1, one launch (start us, length us, event | category | flops | bytes accessed | tf_op | source)
XLA Modules:
  0.0 321.8 jit_solution(16371139674127357684)
XLA Ops:
  13.7 47.3 %all-gather.3.cloned.1.call-done = bf16[128,8192]{0,1:T(8,128)(2,1)} async-done(((bf16[128,1024]{0,1:T(8,128)(2,1)}), bf16[128,8192]{0,1:T(8,128)(2,1)}) %all-gather.3.cloned.1.call-update) | async-done | bytes 2097168 | tf_op jit(solution)/shard_map/all_gather | solution.py:12
  61.0 3.2 copy.130
  74.0 2.5 fusion.6
  87.4 11.9 %all-gather.5.cloned.1.call-done = bf16[7,20,128,128]{3,2,1,0:T(8,128)(2,1)} async-done(((bf16[7,20,32,128]{3,2,1,0:T(8,128)(2,1)}), bf16[7,20,128,128]{3,2,1,0:T(8,128)(2,1)}) %all-gather.5.cloned.1.call-update) | async-done | bytes 4587536 | tf_op jit(solution)/shard_map/all_gather | solution.py:15
  99.3 7.2 %copy.131 = bf16[7,20,128,128]{2,3,1,0:T(8,128)(2,1)} copy(bf16[7,20,128,128]{3,2,1,0:T(8,128)(2,1)} %all-gather.5.cloned.1.call-done) | data formatting | bytes 9175040 | tf_op jit(solution)/shard_map/all_gather | solution.py:15
  106.5 6.9 %select_convert_fusion = (bf16[7,20,128,128]{2,3,1,0:T(8,128)(2,1)}, bf16[7,20,128,128]{2,3,1,0:T(8,128)(2,1)S(1)}) fusion(bf16[7,20,128,128]{2,3,1,0:T(8,128)(2,1)} %fusion, pred[7,20]{1,0:T(8,128)(4,1)S(1)} %iota_compare_fusion, bf16[7,20,128,128]{2,3,1,0:T(8,128)(2,1)} %copy.131), kind=kLoop, calls=%fused_computation.14 | loop fusion | flops 4587520 | bytes 18350220 | tf_op jit(solution)/shard_map/convert_element_type | solution.py:45
  121.7 2.8 copy.141
  124.5 2.8 copy.144
  127.3 2.8 copy.147
  130.0 2.8 copy.150
  136.4 2.4 broadcast_in_dim.47
  138.9 6.8 %scatter_fusion = f32[128,64,128]{2,0,1:T(8,128)} fusion(f32[128,64,128]{2,0,1:T(8,128)} %broadcast_in_dim.47, s32[20]{0:T(128)S(1)} %get-tuple-element.31, f32[20,128,128]{2,1,0:T(8,128)} %copy.141), kind=kCustom, calls=%fused_computation.7 | custom fusion | flops 327680 | bytes 3932240 | tf_op jit(solution)/shard_map/scatter-add | solution.py:31
  145.7 6.9 %scatter_fusion.1 = f32[128,64,128]{2,0,1:T(8,128)} fusion(f32[128,64,128]{2,0,1:T(8,128)} %scatter_fusion, s32[20]{0:T(128)S(1)} %get-tuple-element.32, f32[20,128,128]{2,1,0:T(8,128)} %copy.144), kind=kCustom, calls=%fused_computation.8 | custom fusion | flops 327680 | bytes 3932240 | tf_op jit(solution)/shard_map/scatter-add | solution.py:31
  152.6 7.0 %scatter_fusion.2 = f32[128,64,128]{2,0,1:T(8,128)} fusion(f32[128,64,128]{2,0,1:T(8,128)} %scatter_fusion.1, s32[20]{0:T(128)S(1)} %get-tuple-element.33, f32[20,128,128]{2,1,0:T(8,128)} %copy.147), kind=kCustom, calls=%fused_computation.9 | custom fusion | flops 327680 | bytes 3932240 | tf_op jit(solution)/shard_map/scatter-add | solution.py:31
  159.6 6.9 %scatter_fusion.3 = f32[128,64,128]{2,0,1:T(8,128)} fusion(f32[128,64,128]{2,0,1:T(8,128)} %scatter_fusion.2, s32[20]{0:T(128)S(1)} %get-tuple-element.34, f32[20,128,128]{2,1,0:T(8,128)} %copy.150), kind=kCustom, calls=%fused_computation.10 | custom fusion | flops 327680 | bytes 3932240 | tf_op jit(solution)/shard_map/scatter-add | solution.py:31
  166.5 6.9 %scatter_fusion.4 = f32[128,64,128]{2,0,1:T(8,128)} fusion(f32[128,64,128]{2,0,1:T(8,128)} %scatter_fusion.3, s32[20]{0:T(128)S(1)} %get-tuple-element.35, f32[20,128,128]{2,1,0:T(8,128)} %copy.153), kind=kCustom, calls=%fused_computation.11 | custom fusion | flops 327680 | bytes 3932240 | tf_op jit(solution)/shard_map/scatter-add | solution.py:31
  173.4 6.3 %scatter_fusion.5 = f32[128,64,128]{2,0,1:T(8,128)} fusion(f32[128,64,128]{2,0,1:T(8,128)} %scatter_fusion.4, s32[20]{0:T(128)S(1)} %get-tuple-element.36, f32[20,128,128]{2,1,0:T(8,128)S(1)} %copy.156), kind=kCustom, calls=%fused_computation.12 | custom fusion | flops 327680 | bytes 3932240 | tf_op jit(solution)/shard_map/scatter-add | solution.py:31
  179.7 6.4 %scatter_fusion.6 = f32[128,64,128]{2,0,1:T(8,128)} fusion(f32[128,64,128]{2,0,1:T(8,128)} %scatter_fusion.5, s32[20]{0:T(128)S(1)} %get-tuple-element.30, f32[20,128,128]{2,1,0:T(8,128)S(1)} %copy.159), kind=kCustom, calls=%fused_computation.13 | custom fusion | flops 327680 | bytes 3932240 | tf_op jit(solution)/shard_map/scatter-add | solution.py:31
  186.0 2.6 convert_element_type.15
  188.6 2.9 copy.160
  191.6 7.9 %copy.175 = bf16[7,20,128,128]{3,0,1,2:T(8,128)(2,1)} copy(bf16[7,20,128,128]{2,3,1,0:T(8,128)(2,1)} %get-tuple-element.49) | data formatting | bytes 9175040 | tf_op jit(solution)/shard_map/convert_element_type | solution.py:45
  212.3 45.2 %reduce-scatter.3.cloned.1.call-done = bf16[128,1024]{0,1:T(8,128)(2,1)} async-done(((bf16[128,8192]{0,1:T(8,128)(2,1)}), bf16[128,1024]{0,1:T(8,128)(2,1)}) %reduce-scatter.3.cloned.1.call-update) | async-done | bytes 262160 | tf_op jit(solution)/shard_map/reduce_scatter | solution.py:38
  259.3 52.9 %reduce-scatter.5.cloned.1.call-done = bf16[7,20,32,128]{3,0,1,2:T(8,128)(2,1)} async-done(((bf16[7,20,128,128]{3,0,1,2:T(8,128)(2,1)}), bf16[7,20,32,128]{3,0,1,2:T(8,128)(2,1)}) %reduce-scatter.5.cloned.1.call-update) | async-done | bytes 1146896 | tf_op jit(solution)/shard_map/reduce_scatter | solution.py:44
  312.1 3.1 copy.178
  (75 shorter events, 53.4 us)
Async XLA Ops:
  7.2 53.8 %all-gather.3.cloned.1.call-start = ((), (), s32[]{:S(2)}) async-start(), calls=%async_computation.2 | async-start | bytes 2359296 | tf_op jit(solution)/shard_map/all_gather | solution.py:12
  9.0 90.3 %all-gather.5.cloned.1.call-start = ((), (), s32[]{:S(2)}) async-start(), calls=%async_computation.3 | async-start | bytes 5734400 | tf_op jit(solution)/shard_map/all_gather | solution.py:15
  9.8 247.7 %reduce-scatter.3.cloned.1.call-start = ((), (), s32[]{:S(2)}) async-start(), calls=%async_computation.4 | async-start | bytes 2359296 | tf_op jit(solution)/shard_map/reduce_scatter | solution.py:38
  11.9 62.1 %copy-start.11 = (pred[20]{0:T(512)(128)(4,1)}, pred[20]{0:T(512)(128)(4,1)S(1)}, u32[]{:S(2)}) copy-start(pred[20]{0:T(512)(128)(4,1)S(1)} %get-tuple-element.45) | copy-start | bytes 64
  11.9 64.5 %copy-start.9 = (pred[20]{0:T(512)(128)(4,1)}, pred[20]{0:T(512)(128)(4,1)S(1)}, u32[]{:S(2)}) copy-start(pred[20]{0:T(512)(128)(4,1)S(1)} %get-tuple-element.43) | copy-start | bytes 64
  74.0 9.6 %copy-start.3 = (bf16[20,128,128]{2,1,0:T(8,128)(2,1)S(1)}, bf16[20,128,128]{2,1,0:T(8,128)(2,1)}, u32[]{:S(2)}) copy-start(bf16[20,128,128]{2,1,0:T(8,128)(2,1)} %gather_fusion.4) | copy-start | bytes 1966084
  76.4 8.4 %copy-start.1 = (bf16[20,128,128]{2,1,0:T(8,128)(2,1)S(1)}, bf16[20,128,128]{2,1,0:T(8,128)(2,1)}, u32[]{:S(2)}) copy-start(bf16[20,128,128]{2,1,0:T(8,128)(2,1)} %gather_fusion.5) | copy-start | bytes 1966084
  113.5 6.7 %copy-start = (bf16[7,20,128,128]{2,3,1,0:T(8,128)(2,1)}, bf16[7,20,128,128]{2,3,1,0:T(8,128)(2,1)S(1)}, u32[]{:S(2)}) copy-start(bf16[7,20,128,128]{2,3,1,0:T(8,128)(2,1)S(1)} %get-tuple-element.50) | copy-start | bytes 13762564
  191.5 120.6 %reduce-scatter.5.cloned.1.call-start = ((), (), s32[]{:S(2)}) async-start(), calls=%async_computation.5 | async-start | bytes 6553600 | tf_op jit(solution)/shard_map/reduce_scatter | solution.py:44
  199.5 1.1 copy-start.8
  199.5 1.1 copy-start.12
  199.5 2.7 copy-start.7
  199.5 2.7 copy-start.10
  199.5 4.3 %copy-start.6 = (bf16[20,128,128]{2,1,0:T(8,128)(2,1)S(1)}, bf16[20,128,128]{2,1,0:T(8,128)(2,1)}, u32[]{:S(2)}) copy-start(bf16[20,128,128]{2,1,0:T(8,128)(2,1)} %gather_fusion.2) | copy-start | bytes 1966084
  200.5 4.8 %copy-start.5 = (bf16[20,128,128]{2,1,0:T(8,128)(2,1)S(1)}, bf16[20,128,128]{2,1,0:T(8,128)(2,1)}, u32[]{:S(2)}) copy-start(bf16[20,128,128]{2,1,0:T(8,128)(2,1)} %gather_fusion.3) | copy-start | bytes 1966084
  200.5 6.3 %copy-start.4 = (bf16[20,128,128]{2,1,0:T(8,128)(2,1)S(1)}, bf16[20,128,128]{2,1,0:T(8,128)(2,1)}, u32[]{:S(2)}) copy-start(bf16[20,128,128]{2,1,0:T(8,128)(2,1)} %gather_fusion.4) | copy-start | bytes 1966084
  202.2 6.2 %copy-start.2 = (bf16[20,128,128]{2,1,0:T(8,128)(2,1)S(1)}, bf16[20,128,128]{2,1,0:T(8,128)(2,1)}, u32[]{:S(2)}) copy-start(bf16[20,128,128]{2,1,0:T(8,128)(2,1)} %gather_fusion.5) | copy-start | bytes 1966084
Sparse Core Ops, SparseCore 0:
  10.7 50.2 all-gather.2
  62.6 36.7 all-gather.4
  191.6 65.7 reduce-scatter.2
  259.9 52.2 reduce-scatter.4
where the time goes:
time: 324 us; the launch traced here: 322 us
  waiting for transfers between devices  158 us (49%)
  other arithmetic  59.3 us (18%)
  local copies, waits for them, and re-layouts  57.9 us (18%)
  matrix products  32.4 us (10%)
  between operations  14 us (4%)
    reduce_scatter x1, waiting for transfers between devices, shards(): lax.psum_scatter(stacked.astype(jnp.bfloat16), 'dp', scatter_dimension=2,...  52.9 us
    all_gather x1, waiting for transfers between devices, shards(): whole = lax.all_gather(acts, 'mp', axis=1, tiled=True)  47.3 us
    scatter-add x7, other arithmetic, shards(): partial_value = partial_value.at[:, block_rows[column]].add(contrib)  47.1 us
    reduce_scatter x1, waiting for transfers between devices, shards(): lax.psum_scatter(rounded_partial, 'mp', scatter_dimension=1, tiled=True)  45.2 us
    dot_general x7, local copies, waits for them, and re-layouts, shards(): jnp.einsum('tj,kij->tki', upstream, masked[column], preferred_element_typ...  14.8 us
    dot_general x7, matrix products, shards(): jnp.einsum('tki,tj->kij', picked, upstream, preferred_element_type=jnp.fl...  13.4 us
    all_gather x1, waiting for transfers between devices, shards(): weights_all = lax.all_gather(values, 'dp', axis=2, tiled=True)  11.9 us
    dot_general x7, matrix products, shards(): jnp.einsum('tki,kij->tj', picked, masked[column], preferred_element_type=...  10.8 us
  transfers between devices with their start and end apart: 4, of which 4 were waited for; matrix products, arithmetic and copies ran while one was open for 16% of the time, Pallas kernels for 0%

commit v1 on v0

v1 whole, which is shorter than its diff:
```python
import functools

import jax
import jax.numpy as jnp
from jax import lax
from jax.experimental import pallas as pl
from jax.experimental.pallas import tpu as pltpu
from jax.sharding import PartitionSpec as P

MESH = pl.DeviceIdType.MESH
BF16 = jnp.bfloat16
F32 = jnp.float32
N_Z = 4


def select(rows_in, lanes, width, shift):
    src = lax.broadcasted_iota(jnp.int32, (rows_in, lanes), 0)
    dst = lax.broadcasted_iota(jnp.int32, (rows_in, lanes), 1)
    hit = src == (dst // width) * 128 + shift + dst % width
    return jnp.where(hit, 1.0, 0.0).astype(BF16)


def kernel(
    nd, nm,
    acts_ref, gout_ref, w,
    hid_out, ga_out, flip, gall,
    perm, act, part, ry, rz, hid, hsend, hrecv, tot, garecv,
    aa_s, aa_r, go_s, go_r, az_s, az_r, ay_s, ay_r,
    py_s, py_r, pz_s, pz_r, hd_s, hd_r, ga_s, ga_r,
):
    nz = N_Z
    ny = nm // nz
    d = lax.axis_index("dp")
    m = lax.axis_index("mp")
    z = m // ny
    y = m % ny
    tok, local = acts_ref.shape
    ff = gout_ref.shape[1]
    blk = 128
    feat = act.shape[3]
    local_blocks = local // blk
    width = feat // local_blocks
    group = min(local_blocks, blk // width)
    gw = group * width
    n_group = local_blocks // group

    def dpeer(o):
        return (lax.rem(d + o, nd), m)

    def mpeer(zz, yy):
        return (d, zz * ny + yy)

    def zo(o):
        return lax.rem(z + o + nz, nz)

    def yo(o):
        return lax.rem(y + o + ny, ny)

    def rcopy(src, dst, ss, rs, dev):
        return pltpu.make_async_remote_copy(
            src_ref=src, dst_ref=dst, send_sem=ss, recv_sem=rs, device_id=dev, device_id_type=MESH
        )

    barrier = pltpu.get_barrier_semaphore()
    peers = [dpeer(o) for o in range(1, nd)]
    peers += [mpeer(zo(o), y) for o in range(1, nz)]
    peers += [mpeer(z, yo(b)) for b in range(1, ny)]
    for peer in peers:
        pl.semaphore_signal(barrier, inc=1, device_id=peer, device_id_type=MESH)

    for dd in range(nd):
        pick = select(group * blk, gw, width, dd * width)
        for q in range(n_group):
            got = jnp.dot(
                acts_ref[:, q * group * blk:(q + 1) * group * blk], pick, preferred_element_type=F32
            )
            perm[dd, :, q * gw:(q + 1) * gw] = got.astype(BF16)

    pl.semaphore_wait(barrier, len(peers))

    acts_sent = []
    for o in range(1, nd):
        c = rcopy(perm.at[lax.rem(d + o, nd)], act.at[m, d], aa_s.at[o], aa_r.at[o], dpeer(o))
        c.start()
        acts_sent.append(c)
    gout_sent = []
    for o in range(1, nd):
        c = rcopy(gout_ref, gall.at[d], go_s.at[o], go_r.at[o], dpeer(o))
        c.start()
        gout_sent.append(c)
    act[m, d] = perm[d]
    gall[d] = gout_ref[...]

    for c in acts_sent:
        c.wait_recv()

    sends = []
    for o in range(1, nz):
        c = rcopy(act.at[m], act.at[m], az_s.at[o], az_r.at[o], mpeer(zo(o), y))
        c.start()
        sends.append(c)

    def spread(s):
        chunk = zo(-s) * ny + y
        for b in range(1, ny):
            c = rcopy(act.at[chunk], act.at[chunk], ay_s.at[s, b], ay_r.at[s, b], mpeer(z, yo(b)))
            c.start()
            sends.append(c)

    spread(0)

    for c in gout_sent:
        c.wait_recv()

    def weights(mm):
        return w[pl.ds(pl.multiple_of(mm * feat, feat), feat), :].astype(BF16)

    def partial(mm):
        wm = weights(mm)

        @pl.loop(0, nd)
        def _(t):
            part[mm, t] = lax.dot_general(
                gall[t], wm, (((1,), (1,)), ((), ())), preferred_element_type=F32
            ).astype(BF16)

    for a in range(1, nz + 1):
        zt = zo(a % nz)
        for b in range(1, ny):
            mm = zt * ny + yo(b)
            partial(mm)
            c = rcopy(part.at[mm], ry.at[a - 1, b - 1], py_s.at[a - 1, b], py_r.at[a - 1, b], mpeer(z, yo(b)))
            c.start()
            sends.append(c)
        if a < nz:
            rcopy(act.at[m], act.at[m], az_s.at[a], az_r.at[a], mpeer(zo(a), y)).wait_recv()
            spread(a)
        partial(zt * ny + y)

    hid[...] = jnp.zeros_like(hid)

    def use(mm):
        wm = weights(mm)

        @pl.loop(0, nd)
        def _(t):
            hid[t] += jnp.dot(act[mm, t], wm, preferred_element_type=F32)

        flip[pl.ds(pl.multiple_of(mm * feat, feat), feat), :] = (
            act[mm].reshape(nd * tok, feat).T.astype(flip.dtype)
        )

    for a in range(1, nz + 1):
        zt = zo(a % nz)
        mm = zt * ny + y
        for b in range(1, ny):
            rcopy(part.at[mm], ry.at[a - 1, b - 1], py_s.at[a - 1, b], py_r.at[a - 1, b], mpeer(z, yo(b))).wait_recv()

        @pl.loop(0, nd)
        def _(t):
            total = part[mm, t].astype(F32)
            for b in range(1, ny):
                total += ry[a - 1, b - 1, t].astype(F32)
            part[mm, t] = total.astype(BF16)

        if a < nz:
            c = rcopy(part.at[mm], rz.at[a - 1], pz_s.at[a], pz_r.at[a], mpeer(zt, y))
            c.start()
            sends.append(c)
        use(zo(-(a % nz)) * ny + y)

    for s in range(nz):
        for b in range(1, ny):
            chunk = zo(-s) * ny + yo(-b)
            rcopy(act.at[chunk], act.at[chunk], ay_s.at[s, b], ay_r.at[s, b], mpeer(z, yo(b))).wait_recv()
            use(chunk)

    @pl.loop(0, nd)
    def _(t):
        hsend[t] = hid[t].astype(BF16)

    hid_sent = []
    for o in range(1, nd):
        c = rcopy(hsend.at[lax.rem(d + o, nd)], hrecv.at[o - 1], hd_s.at[o], hd_r.at[o], dpeer(o))
        c.start()
        hid_sent.append(c)

    for a in range(1, nz):
        rcopy(part.at[m], rz.at[a - 1], pz_s.at[a], pz_r.at[a], mpeer(zo(a), y)).wait_recv()

    @pl.loop(0, nd)
    def _(t):
        total = part[m, t].astype(F32)
        for a in range(1, nz):
            total += rz[a - 1, t].astype(F32)
        tot[t] = total.astype(BF16)

    ga_sent = []
    for o in range(1, nd):
        c = rcopy(tot.at[lax.rem(d + o, nd)], garecv.at[d], ga_s.at[o], ga_r.at[o], dpeer(o))
        c.start()
        ga_sent.append(c)
    garecv[d] = tot[d]

    for c in hid_sent:
        c.wait_recv()
    total = hid[d]
    for o in range(1, nd):
        total += hrecv[o - 1].astype(F32)
    hid_out[...] = total.astype(BF16)

    for c in ga_sent:
        c.wait_recv()
    for q in range(n_group):
        total = jnp.zeros((tok, group * blk), F32)
        for dd in range(nd):
            pick = select(group * blk, gw, width, dd * width)
            total += lax.dot_general(
                garecv[dd, :, q * gw:(q + 1) * gw], pick, (((1,), (1,)), ((), ())),
                preferred_element_type=F32,
            )
        ga_out[:, q * group * blk:(q + 1) * group * blk] = total.astype(BF16)

    for c in acts_sent + gout_sent + sends + hid_sent + ga_sent:
        c.wait_send()


def densify(rows_ref, count_ref, val_ref, w_ref):
    c = pl.program_id(0)
    slots, width = val_ref.shape[1:3]
    w_ref[...] = jnp.zeros_like(w_ref)

    @pl.loop(0, slots)
    def _(k):
        @pl.when(k < count_ref[c])
        def _():
            start = pl.multiple_of(rows_ref[c, k] * width, width)
            w_ref[pl.ds(start, width), :] = val_ref[0, k]


def weight_grad(rows_ref, count_ref, flip_ref, gout_ref, gv_ref, picked):
    c = pl.program_id(0)
    nd, tok, blk = gout_ref.shape
    slots, width = gv_ref.shape[1:3]

    for k in range(slots):
        live = k < count_ref[c]
        start = pl.multiple_of(jnp.where(live, rows_ref[c, k], 0) * width, width)
        picked[k * width:(k + 1) * width, :] = flip_ref[pl.ds(start, width), :]
    got = jnp.dot(
        picked[...].astype(BF16), gout_ref[...].reshape(nd * tok, blk), preferred_element_type=F32
    ).reshape(slots, width, blk)
    slot = lax.broadcasted_iota(jnp.int32, got.shape, 0)
    gv_ref[0] = jnp.where(slot < count_ref[c], got, 0.0)


def shards(nd, nm, acts, grad_out, values, block_rows, block_count):
    tok, local = acts.shape
    ff = grad_out.shape[1]
    cols, slots, width, blk = values.shape
    nz = N_Z
    ny = nm // nz
    local_blocks = local // blk
    feat = local_blocks * width
    depth = feat * nm
    if width % 16:
        values = values.astype(F32)
    dma = pltpu.SemaphoreType.DMA
    vmem = pl.BlockSpec(memory_space=pltpu.VMEM)
    smem = pl.BlockSpec(memory_space=pltpu.SMEM)
    limit = 62 * 2 ** 20
    dense = pl.pallas_call(
        densify,
        grid=(cols,),
        out_shape=jax.ShapeDtypeStruct((depth, ff), values.dtype),
        in_specs=[smem, smem, pl.BlockSpec((1, slots, width, blk), lambda c: (c, 0, 0, 0))],
        out_specs=pl.BlockSpec((depth, blk), lambda c: (0, c)),
        compiler_params=pltpu.CompilerParams(vmem_limit_bytes=limit),
    )(block_rows, block_count, values)
    hidden_out, grad_acts, flip, gall = pl.pallas_call(
        functools.partial(kernel, nd, nm),
        out_shape=(
            jax.ShapeDtypeStruct((tok, ff), BF16),
            jax.ShapeDtypeStruct((tok, local), BF16),
            jax.ShapeDtypeStruct((depth, nd * tok), values.dtype),
            jax.ShapeDtypeStruct((nd, tok, ff), BF16),
        ),
        in_specs=[vmem] * 3,
        out_specs=(vmem,) * 4,
        scratch_shapes=[
            pltpu.VMEM((nd, tok, feat), BF16),
            pltpu.VMEM((nm, nd, tok, feat), BF16),
            pltpu.VMEM((nm, nd, tok, feat), BF16),
            pltpu.VMEM((nz, ny - 1, nd, tok, feat), BF16),
            pltpu.VMEM((nz - 1, nd, tok, feat), BF16),
            pltpu.VMEM((nd, tok, ff), F32),
            pltpu.VMEM((nd, tok, ff), BF16),
            pltpu.VMEM((nd - 1, tok, ff), BF16),
            pltpu.VMEM((nd, tok, feat), BF16),
            pltpu.VMEM((nd, tok, feat), BF16),
            dma((nd,)), dma((nd,)), dma((nd,)), dma((nd,)),
            dma((nz,)), dma((nz,)), dma((nz, ny)), dma((nz, ny)),
            dma((nz, ny)), dma((nz, ny)), dma((nz,)), dma((nz,)),
            dma((nd,)), dma((nd,)), dma((nd,)), dma((nd,)),
        ],
        compiler_params=pltpu.CompilerParams(
            collective_id=0, has_side_effects=True, vmem_limit_bytes=limit
        ),
        cost_estimate=pl.CostEstimate(
            flops=4 * nd * tok * depth * ff, bytes_accessed=2 ** 23, transcendentals=0
        ),
    )(acts, grad_out, dense)
    grad_values = pl.pallas_call(
        weight_grad,
        grid=(cols,),
        out_shape=jax.ShapeDtypeStruct(values.shape, F32),
        in_specs=[
            smem, smem,
            pl.BlockSpec((depth, nd * tok), lambda c: (0, 0)),
            pl.BlockSpec((nd, tok, blk), lambda c: (0, 0, c)),
        ],
        out_specs=pl.BlockSpec((1, slots, width, blk), lambda c: (c, 0, 0, 0)),
        scratch_shapes=[pltpu.VMEM((slots * width, nd * tok), values.dtype)],
        compiler_params=pltpu.CompilerParams(vmem_limit_bytes=limit),
    )(block_rows, block_count, flip, gall)
    return hidden_out, grad_acts, grad_values


def solution(mesh):
    placed = (P("dp", "mp"), P("dp", "mp"), P("mp", None, "dp", None), P("mp", None), P("mp"))
    return jax.shard_map(
        functools.partial(shards, mesh.shape["dp"], mesh.shape["mp"]),
        mesh=mesh,
        in_specs=placed,
        out_specs=(P("dp", "mp"), P("dp", "mp"), P("mp", None, "dp", None)),
        check_vma=False,
    )
```

time: 324 us -> 97.5 us (0.30)
  waiting for transfers between devices: 158 us -> 0 us
  Pallas kernels: 0 us -> 95.1 us
  other arithmetic: 59.3 us -> 0 us
  local copies, waits for them, and re-layouts: 57.9 us -> 1.4 us
  matrix products: 32.4 us -> 0 us
  between operations: 14 us -> 0.66 us
    reduce_scatter x2 -> x0, waiting for transfers between devices: 98 us -> none  [the longest x1 52.9 us: shards(): lax.psum_scatter(stacked.astype(jnp.bfloat16), 'dp', scatter_dimension=2,...]
    pallas_call x0 -> x3, Pallas kernels: none -> 95.1 us  [the longest x1 81.3 us: shards(): pl.pallas_call(functools.partial(kernel, nd, nm), out_shape=(jax.ShapeDty...]
    all_gather x2 -> x0, waiting for transfers between devices: 59.2 us -> none  [the longest x1 47.3 us: shards(): whole = lax.all_gather(acts, 'mp', axis=1, tiled=True)]
    scatter-add x7 -> x0, other arithmetic: 47.1 us -> none  [shards(): partial_value = partial_value.at[:, block_rows[column]].add(contrib)]
    dot_general x21 -> x0, matrix products: 32.4 us -> none  [the longest x7 13.4 us: shards(): jnp.einsum('tki,tj->kij', picked, upstream, preferred_element_type=jnp.fl...]
    dot_general x7 -> x0, local copies, waits for them, and re-layouts: 14.8 us -> none  [shards(): jnp.einsum('tj,kij->tki', upstream, masked[column], preferred_element_typ...]
    convert_element_type x2 -> x0, local copies, waits for them, and re-layouts: 10.8 us -> none  [the longest x1 7.9 us: shards(): stacked.astype(jnp.bfloat16)]
    gather x7 -> x0, local copies, waits for them, and re-layouts: 9.73 us -> none  [shards(): picked = jnp.take(blocked, block_rows[column], axis=1)]
  transfers between devices with their start and end apart: 4 -> 0, of which waited for: 4 -> 0; matrix products, arithmetic and copies ran while one was open for 16% -> 0% of each run, Pallas kernels for 0% -> 0%
where the time goes in v1:
time: 97.5 us; the launch traced here: 97.1 us
  Pallas kernels  95.1 us (98%)
  local copies, waits for them, and re-layouts  1.4 us (1%)
    pallas_call x1, Pallas kernels, shards(): pl.pallas_call(functools.partial(kernel, nd, nm), out_shape=(jax.ShapeDty...  81.3 us
    pallas_call x1, Pallas kernels, shards(): pl.pallas_call(weight_grad, grid=(cols,), out_shape=jax.ShapeDtypeStruct(...  6.97 us
    pallas_call x1, Pallas kernels, shards(): pl.pallas_call(densify, grid=(cols,), out_shape=jax.ShapeDtypeStruct((dep...  6.8 us

profile of v1, /device:TPU:1, one launch (start us, length us, event | category | flops | bytes accessed | tf_op | source)
XLA Modules:
  0.0 97.1 jit_solution(9115942441261910362)
XLA Ops:
  0.6 6.8 %shard_map.76.w = bf16[2048,896]{1,0:T(8,128)(2,1)} custom-call(s32[7,20]{1,0:T(8,128)} %rows_ref.3, s32[7]{0:T(128)} %count_ref.3, bf16[7,20,32,128]{3,2,1,0:T(8,128)(2,1)} %val_ref.1), custom_call_target="tpu_custom_call" | custom-call | tf_op jit(solution)/shard_map/pallas_call | solution.py:272
  7.4 81.3 %shard_map.77 = (bf16[128,896]{1,0:T(8,128)(2,1)}, bf16[128,1024]{1,0:T(8,128)(2,1)}, bf16[2048,512]{1,0:T(8,128)(2,1)}, bf16[4,128,896]{2,1,0:T(8,128)(2,1)}) custom-call(bf16[128,1024]{1,0:T(8,128)(2,1)} %acts_ref.1, bf16[128,896]{1,0:T(8,128)(2,1)} %gout_ref.1, bf16[2048,896]{1,0:T(8,128)(2,1)} %shard_map.76.w), custom_call_target="tpu_custom_call" | custom-call | flops 3758096384 | bytes 8388608 | tf_op jit(solution)/shard_map/pallas_call | solution.py:280
  88.7 0.0 copy-start.1
  88.7 0.0 copy-start
  88.7 7.0 %shard_map.78 = f32[7,20,32,128]{3,2,1,0:T(8,128)} custom-call(s32[7,20]{1,0:T(8,128)} %rows_ref.3, s32[7]{0:T(128)} %count_ref.3, bf16[2048,512]{1,0:T(8,128)(2,1)} %get-tuple-element.9.flip_ref, bf16[4,128,896]{2,1,0:T(8,128)(2,1)} %get-tuple-element.10.gout_ref), custom_call_target="tpu_custom_call" | custom-call | tf_op jit(solution)/shard_map/pallas_call | solution.py:313
  95.7 0.0 copy-done.1
  95.7 0.7 copy.10
  96.4 0.0 copy-done
  96.4 0.7 copy.11
Async XLA Ops:
  88.7 7.0 %copy-start.1 = (bf16[128,896]{1,0:T(8,128)(2,1)S(1)}, bf16[128,896]{1,0:T(8,128)(2,1)}, u32[]{:S(2)}) copy-start(bf16[128,896]{1,0:T(8,128)(2,1)} %get-tuple-element.14) | copy-start | bytes 688132
  88.7 7.7 %copy-start = (bf16[128,1024]{1,0:T(8,128)(2,1)S(1)}, bf16[128,1024]{1,0:T(8,128)(2,1)}, u32[]{:S(2)}) copy-start(bf16[128,1024]{1,0:T(8,128)(2,1)} %get-tuple-element.15) | copy-start | bytes 786436

commit v2 on v1

v2 whole, which is shorter than its diff:
```python
import functools

import jax
import jax.numpy as jnp
from jax import lax
from jax.experimental import pallas as pl
from jax.experimental.pallas import tpu as pltpu
from jax.sharding import PartitionSpec as P

MESH = pl.DeviceIdType.MESH
BF16 = jnp.bfloat16
F32 = jnp.float32
N_Z = 4


def select(rows_in, lanes, width, shift):
    src = lax.broadcasted_iota(jnp.int32, (rows_in, lanes), 0)
    dst = lax.broadcasted_iota(jnp.int32, (rows_in, lanes), 1)
    hit = src == (dst // width) * 128 + shift + dst % width
    return jnp.where(hit, 1.0, 0.0).astype(BF16)


def kernel(
    nd, nm,
    rows_ref, slot_ref, acts_ref, gout_ref, val_hbm,
    hid_out, ga_out, gv_out,
    val, w, flip, gall, picked,
    perm, act, part, ry, rz, hid, hsend, hrecv, tot, gasend, garecv,
    val_s, aa_s, aa_r, go_s, go_r, gf_s, gf_r, az_s, az_r, ay_s, ay_r,
    py_s, py_r, pz_s, pz_r, hd_s, hd_r, ga_s, ga_r,
):
    nz = N_Z
    ny = nm // nz
    half = nd // 2
    d = lax.axis_index("dp")
    m = lax.axis_index("mp")
    z = m // ny
    y = m % ny
    h = d // 2
    core = d % 2
    twin = (h * 2 + 1 - core, m)
    tok, local = acts_ref.shape
    ff = gout_ref.shape[1]
    cols, slots, width, blk = val_hbm.shape
    feat = act.shape[3]
    local_blocks = local // blk
    group = min(local_blocks, blk // width)
    gw = group * width
    n_group = local_blocks // group
    row_blocks = local_blocks * nm

    def dpeer(o):
        return (lax.rem(d + o, nd), m)

    def hpeer(o):
        return (lax.rem(h + o, half) * 2 + core, m)

    def mpeer(zz, yy):
        return (d, zz * ny + yy)

    def yo(o):
        return lax.rem(y + o + ny, ny)

    def rcopy(src, dst, ss, rs, dev):
        return pltpu.make_async_remote_copy(
            src_ref=src, dst_ref=dst, send_sem=ss, recv_sem=rs, device_id=dev, device_id_type=MESH
        )

    load = pltpu.make_async_copy(val_hbm, val.at[:, 0:slots], val_s)
    load.start()

    barrier = pltpu.get_barrier_semaphore()
    peers = [dpeer(o) for o in range(1, nd)]
    peers += [mpeer(z, yo(b)) for b in range(1, ny)]

    def greet(peer):
        pl.semaphore_signal(barrier, inc=1, device_id=peer, device_id_type=MESH)

    for peer in peers:
        greet(peer)

    @pl.when(z > 0)
    def _():
        greet(mpeer(z - 1, y))

    @pl.when(z < nz - 1)
    def _():
        greet(mpeer(z + 1, y))

    for dd in range(nd):
        pick = select(group * blk, gw, width, dd * width)
        for q in range(n_group):
            got = jnp.dot(
                acts_ref[:, q * group * blk:(q + 1) * group * blk], pick, preferred_element_type=F32
            )
            perm[dd, :, q * gw:(q + 1) * gw] = got.astype(BF16)

    ends = (z == 0).astype(jnp.int32) + (z == nz - 1).astype(jnp.int32)
    pl.semaphore_wait(barrier, len(peers) + 2 - ends)

    sends = []

    def go(c):
        c.start()
        sends.append(c)
        return c

    acts_sent = [
        go(rcopy(perm.at[lax.rem(d + o, nd)], act.at[m, d], aa_s.at[o], aa_r.at[o], dpeer(o)))
        for o in range(1, nd)
    ]
    gout_sent = [
        go(rcopy(gout_ref, gall.at[d], go_s.at[o], go_r.at[o], hpeer(o))) for o in range(1, half)
    ]
    gout_twin = [go(rcopy(gout_ref, gall.at[d], gf_s.at[0], gf_r.at[0], twin))]
    act[m, d] = perm[d]
    gall[d] = gout_ref[...]

    load.wait()
    for c in range(cols):
        val[c, slots] = jnp.zeros((width, blk), val.dtype)

    @pl.loop(0, row_blocks, unroll=2)
    def _(r):
        for c in range(cols):
            w[pl.ds(pl.multiple_of(r * width, width), width), c * blk:(c + 1) * blk] = val[
                c, slot_ref[c, r]
            ]

    for c in acts_sent:
        c.wait_recv()

    def along(right, src):
        ref = act.at[src * ny + y]
        side = 0 if right else 1
        return rcopy(ref, ref, az_s.at[side, src], az_r.at[side, src], mpeer(z + 1 if right else z - 1, y))

    def across(src, b, back):
        ref = act.at[src * ny + (yo(-b) if back else y)]
        return rcopy(ref, ref, ay_s.at[src, b], ay_r.at[src, b], mpeer(z, yo(b)))

    def spread(src):
        for b in range(1, ny):
            across(src, b, False).start()

    @pl.when(z < nz - 1)
    def _():
        along(True, z).start()

    @pl.when(z > 0)
    def _():
        along(False, z).start()

    spread(z)

    def arrival(s):
        @pl.when(z >= s)
        def _():
            along(True, z - s).wait_recv()

            @pl.when(z < nz - 1)
            def _():
                along(True, z - s).start()

            spread(z - s)

        @pl.when(z + s < nz)
        def _():
            along(False, z + s).wait_recv()

            @pl.when(z > 0)
            def _():
                along(False, z + s).start()

            spread(z + s)

    for o, c in enumerate(gout_sent):
        c.wait_recv()
        ref = gall.at[lax.rem(h - (o + 1) + half, half) * 2 + core]
        gout_twin.append(go(rcopy(ref, ref, gf_s.at[o + 1], gf_r.at[o + 1], twin)))
    for c in gout_twin:
        c.wait_recv()

    def weights(mm):
        return w[pl.ds(pl.multiple_of(mm * feat, feat), feat), :].astype(BF16)

    def partial(mm):
        part[mm] = lax.dot_general(
            gall[...].reshape(nd * tok, ff), weights(mm), (((1,), (1,)), ((), ())),
            preferred_element_type=F32,
        ).astype(BF16).reshape(nd, tok, feat)

    def target(a):
        down = nz - 1 - a
        low = down - (down <= z).astype(jnp.int32)
        high = a + (jnp.int32(a) >= z).astype(jnp.int32)
        return z if a == nz - 1 else jnp.where(z < nz // 2, low, high)

    def to_y(a, b):
        return rcopy(
            part.at[target(a) * ny + yo(b)], ry.at[a, b - 1], py_s.at[a, b], py_r.at[a, b], mpeer(z, yo(b))
        )

    for a in range(nz):
        for b in range(1, ny):
            partial(target(a) * ny + yo(b))
            go(to_y(a, b))
        if a < nz - 1:
            arrival(a + 1)

    @pl.loop(0, nz)
    def _(zz):
        partial(zz * ny + y)

    hid[...] = jnp.zeros_like(hid)

    def use(mm):
        am = act[mm].reshape(nd * tok, feat)
        for lo in range(0, ff, 256):
            hi = min(lo + 256, ff)
            wm = w[pl.ds(pl.multiple_of(mm * feat, feat), feat), lo:hi].astype(BF16)
            hid[:, :, lo:hi] += jnp.dot(am, wm, preferred_element_type=F32).reshape(nd, tok, hi - lo)
        flip[pl.ds(mm * local_blocks, local_blocks)] = am.T.astype(flip.dtype).reshape(
            local_blocks, width, nd * tok
        )

    def sum_y(a):
        mm = target(a) * ny + y
        for b in range(1, ny):
            to_y(a, b).wait_recv()

        @pl.loop(0, nd)
        def _(t):
            total = part[mm, t].astype(F32)
            for b in range(1, ny):
                total += ry[a, b - 1, t].astype(F32)
            part[mm, t] = total.astype(BF16)

    def to_z(zt):
        right = (zt > z).astype(jnp.int32)
        return rcopy(
            part.at[zt * ny + y], rz.at[1 - right, zt], pz_s.at[1 - right, zt], pz_r.at[1 - right, zt],
            mpeer(z + 2 * right - 1, y),
        )

    def from_z(side, zt):
        ref = rz.at[side, zt]
        rcopy(ref, ref, pz_s.at[side, zt], pz_r.at[side, zt], mpeer(z, y)).wait_recv()

    def sum_z(a):
        zt = target(a)
        side = 1 - (zt > z).astype(jnp.int32)
        sum_y(a)

        @pl.when(jnp.where(zt > z, z > 0, z < nz - 1))
        def _():
            from_z(side, zt)

            @pl.loop(0, nd)
            def _(t):
                part[zt * ny + y, t] = (
                    part[zt * ny + y, t].astype(F32) + rz[side, zt, t].astype(F32)
                ).astype(BF16)

        to_z(zt).start()

    def use_far(s):
        src = lax.rem(z + s, nz)
        for b in range(1, ny):
            across(src, b, True).wait_recv()
            use(src * ny + yo(-b))

    sum_z(0)

    @pl.loop(0, nz)
    def _(zz):
        use(zz * ny + y)

    sum_z(1)

    @pl.loop(0, nz)
    def _(s):
        use_far(s)

    @pl.loop(0, nd)
    def _(t):
        hsend[t] = hid[t].astype(BF16)

    hid_sent = [
        go(rcopy(hsend.at[lax.rem(d + o, nd)], hrecv.at[o - 1], hd_s.at[o], hd_r.at[o], dpeer(o)))
        for o in range(1, nd)
    ]
    for a in range(2, nz - 1):
        sum_z(a)
    sum_y(nz - 1)

    for c in range(cols):
        for k in range(slots):
            picked[k * width:(k + 1) * width, :] = flip[rows_ref[c, k]]
        gv_out[c] = jnp.dot(
            picked[...].astype(BF16), gall[:, :, c * blk:(c + 1) * blk].reshape(nd * tok, blk),
            preferred_element_type=F32,
        ).reshape(slots, width, blk)

    @pl.loop(0, nd)
    def _(t):
        tot[t] = part[m, t].astype(F32)

    for side in range(2):
        @pl.when(z > 0 if side == 0 else z < nz - 1)
        def _():
            from_z(side, z)

            @pl.loop(0, nd)
            def _(t):
                tot[t] += rz[side, z, t].astype(F32)

    @pl.loop(0, nd)
    def _(t):
        gasend[t] = tot[t].astype(BF16)

    garecv[d] = gasend[d]

    ga_sent = [
        go(rcopy(gasend.at[lax.rem(d + o, nd)], garecv.at[d], ga_s.at[o], ga_r.at[o], dpeer(o)))
        for o in range(1, nd)
    ]

    for c in hid_sent:
        c.wait_recv()
    total = hid[d]
    for o in range(1, nd):
        total += hrecv[o - 1].astype(F32)
    hid_out[...] = total.astype(BF16)

    for c in ga_sent:
        c.wait_recv()
    for q in range(n_group):
        total = jnp.zeros((tok, group * blk), F32)
        for dd in range(nd):
            pick = select(group * blk, gw, width, dd * width)
            total += lax.dot_general(
                garecv[dd, :, q * gw:(q + 1) * gw], pick, (((1,), (1,)), ((), ())),
                preferred_element_type=F32,
            )
        ga_out[:, q * group * blk:(q + 1) * group * blk] = total.astype(BF16)

    for c in sends:
        c.wait_send()
    for src in range(nz):
        for b in range(1, ny):
            across(src, b, False).wait_send()

        @pl.when((z < nz - 1) & (z >= src))
        def _():
            along(True, src).wait_send()

        @pl.when((z > 0) & (z <= src))
        def _():
            along(False, src).wait_send()
    for a in range(nz - 1):
        to_z(target(a)).wait_send()


def shards(nd, nm, acts, grad_out, values, block_rows, block_count):
    tok, local = acts.shape
    ff = grad_out.shape[1]
    cols, slots, width, blk = values.shape
    nz = N_Z
    ny = nm // nz
    local_blocks = local // blk
    feat = local_blocks * width
    row_blocks = local_blocks * nm
    depth = feat * nm
    live = jnp.arange(slots, dtype=jnp.int32)[None, :] < block_count[:, None]
    hit = (block_rows[:, :, None] == jnp.arange(row_blocks, dtype=jnp.int32)) & live[:, :, None]
    slot_of = jnp.min(
        jnp.where(hit, jnp.arange(slots, dtype=jnp.int32)[None, :, None], slots), axis=1
    )
    if width % 16:
        values = values.astype(F32)
    kind = values.dtype
    dma = pltpu.SemaphoreType.DMA
    vmem = pl.BlockSpec(memory_space=pltpu.VMEM)
    smem = pl.BlockSpec(memory_space=pltpu.SMEM)
    hidden_out, grad_acts, grad_values = pl.pallas_call(
        functools.partial(kernel, nd, nm),
        out_shape=(
            jax.ShapeDtypeStruct((tok, ff), BF16),
            jax.ShapeDtypeStruct((tok, local), BF16),
            jax.ShapeDtypeStruct(values.shape, F32),
        ),
        in_specs=[smem] * 2 + [vmem] * 2 + [pl.BlockSpec(memory_space=pl.ANY)],
        out_specs=(vmem,) * 3,
        scratch_shapes=[
            pltpu.VMEM((cols, slots + 1, width, blk), kind),
            pltpu.VMEM((depth, ff), kind),
            pltpu.VMEM((row_blocks, width, nd * tok), kind),
            pltpu.VMEM((nd, tok, ff), BF16),
            pltpu.VMEM((slots * width, nd * tok), kind),
            pltpu.VMEM((nd, tok, feat), BF16),
            pltpu.VMEM((nm, nd, tok, feat), BF16),
            pltpu.VMEM((nm, nd, tok, feat), BF16),
            pltpu.VMEM((nz, ny - 1, nd, tok, feat), BF16),
            pltpu.VMEM((2, nz, nd, tok, feat), BF16),
            pltpu.VMEM((nd, tok, ff), F32),
            pltpu.VMEM((nd, tok, ff), BF16),
            pltpu.VMEM((nd - 1, tok, ff), BF16),
            pltpu.VMEM((nd, tok, feat), F32),
            pltpu.VMEM((nd, tok, feat), BF16),
            pltpu.VMEM((nd, tok, feat), BF16),
            dma(()),
            dma((nd,)), dma((nd,)), dma((nd,)), dma((nd,)), dma((nd,)), dma((nd,)),
            dma((2, nz)), dma((2, nz)), dma((nz, ny)), dma((nz, ny)),
            dma((nz, ny)), dma((nz, ny)), dma((2, nz)), dma((2, nz)),
            dma((nd,)), dma((nd,)), dma((nd,)), dma((nd,)),
        ],
        compiler_params=pltpu.CompilerParams(
            collective_id=0, has_side_effects=True, vmem_limit_bytes=62 * 2 ** 20
        ),
        cost_estimate=pl.CostEstimate(
            flops=4 * nd * tok * depth * ff, bytes_accessed=2 ** 23, transcendentals=0
        ),
    )(block_rows, slot_of, acts, grad_out, values)
    grad_values = jnp.where(live[:, :, None, None], grad_values, jnp.zeros((), F32))
    return hidden_out, grad_acts, grad_values


def solution(mesh):
    placed = (P("dp", "mp"), P("dp", "mp"), P("mp", None, "dp", None), P("mp", None), P("mp"))
    return jax.shard_map(
        functools.partial(shards, mesh.shape["dp"], mesh.shape["mp"]),
        mesh=mesh,
        in_specs=placed,
        out_specs=(P("dp", "mp"), P("dp", "mp"), P("mp", None, "dp", None)),
        check_vma=False,
    )
```

time: 97.5 us -> 77.9 us (0.80)
  Pallas kernels: 95.1 us -> 69.8 us
  other arithmetic: 0 us -> 4.76 us
    pallas_call x2 -> x0, Pallas kernels: 13.8 us -> none  [the longest x1 6.97 us: shards(): pl.pallas_call(weight_grad, grid=(cols,), out_shape=jax.ShapeDtypeStruct(...]
    pallas_call x1, Pallas kernels: 81.3 us -> 69.8 us  [shards(): pl.pallas_call(functools.partial(kernel, nd, nm), out_shape=(jax.ShapeDty...]
    select_n x0 -> x1, other arithmetic: none -> 3.32 us  [shards(): jnp.where(live[:, :, None, None], grad_values, jnp.zeros((), F32))]
    unnamed x6 -> x7, local copies, waits for them, and re-layouts: 1.4 us -> 2.18 us
where the time goes in v2:
time: 77.9 us; the launch traced here: 77.5 us
  Pallas kernels  69.8 us (90%)
  other arithmetic  4.76 us (6%)
  local copies, waits for them, and re-layouts  2.29 us (3%)
    pallas_call x1, Pallas kernels, shards(): pl.pallas_call(functools.partial(kernel, nd, nm), out_shape=(jax.ShapeDty...  69.8 us
    select_n x1, other arithmetic, shards(): jnp.where(live[:, :, None, None], grad_values, jnp.zeros((), F32))  3.32 us
    unnamed x7, local copies, waits for them, and re-layouts  2.18 us

profile of v2, /device:TPU:1, one launch (start us, length us, event | category | flops | bytes accessed | tf_op | source)
XLA Modules:
  0.0 77.5 jit_solution(13696284886547277402)
XLA Ops:
  0.6 0.7 iota_compare_fusion.1
  1.4 0.1 copy.9
  1.5 0.8 %copy.8 = s32[7,20]{0,1:T(8,128)S(1)} copy(s32[7,20]{1,0:T(8,128)} %rows_ref.1) | data formatting | bytes 1120 | tf_op args[3]
  2.2 0.7 select_reduce_fusion.slot_ref
  3.0 69.8 %shard_map.76 = (bf16[128,896]{1,0:T(8,128)(2,1)}, bf16[128,1024]{1,0:T(8,128)(2,1)}, f32[7,20,32,128]{3,2,1,0:T(8,128)}) custom-call(s32[7,20]{1,0:T(8,128)} %rows_ref.1, s32[7,64]{1,0:T(8,128)} %select_reduce_fusion.slot_ref, bf16[128,1024]{1,0:T(8,128)(2,1)} %acts_ref.1, bf16[128,896]{1,0:T(8,128)(2,1)} %gout_ref.1, bf16[7,20,32,128]{3,2,1,0:T(8,128)(2,1)} %val_hbm.1), custom_call_target="tpu_custom_call" | custom-call | flops 3758096384 | bytes 8388608 | tf_op jit(solution)/shard_map/pallas_call | solution.py:386
  72.7 0.0 copy-start.1
  72.7 0.0 copy-start
  72.8 3.3 %broadcast_select_fusion = f32[7,20,32,128]{3,2,1,0:T(8,128)} fusion(f32[7,20,32,128]{3,2,1,0:T(8,128)} %get-tuple-element.8, pred[7,20]{1,0:T(8,128)(4,1)S(1)} %iota_compare_fusion.1), kind=kLoop, calls=%fused_computation | loop fusion | flops 573440 | bytes 4587660 | tf_op jit(solution)/shard_map/jit(_where)/select_n | solution.py:425
  76.1 0.0 copy-done.1
  76.1 0.7 copy.12
  76.8 0.0 copy-done
  76.8 0.7 copy.13
Async XLA Ops:
  72.7 3.3 %copy-start.1 = (bf16[128,896]{1,0:T(8,128)(2,1)S(1)}, bf16[128,896]{1,0:T(8,128)(2,1)}, u32[]{:S(2)}) copy-start(bf16[128,896]{1,0:T(8,128)(2,1)} %get-tuple-element.12) | copy-start | bytes 688132
  72.7 4.0 %copy-start = (bf16[128,1024]{1,0:T(8,128)(2,1)S(1)}, bf16[128,1024]{1,0:T(8,128)(2,1)}, u32[]{:S(2)}) copy-start(bf16[128,1024]{1,0:T(8,128)(2,1)} %get-tuple-element.13) | copy-start | bytes 786436

commit v3 on v2

--- a/solution.py
+++ b/solution.py
@@ -23,10 +23,10 @@
 def kernel(
     nd, nm,
     rows_ref, slot_ref, acts_ref, gout_ref, val_hbm,
-    hid_out, ga_out, gv_out,
-    val, w, flip, gall, picked,
+    hid_out, ga_out, gv_hbm,
+    val, w, flip, gall, picked, picks, gv,
     perm, act, part, ry, rz, hid, hsend, hrecv, tot, gasend, garecv,
-    val_s, aa_s, aa_r, go_s, go_r, gf_s, gf_r, az_s, az_r, ay_s, ay_r,
+    val_s, gv_s, aa_s, aa_r, go_s, go_r, gf_s, gf_r, az_s, az_r, ay_s, ay_r,
     py_s, py_r, pz_s, pz_r, hd_s, hd_r, ga_s, ga_r,
 ):
     nz = N_Z
@@ -88,10 +88,10 @@
         greet(mpeer(z + 1, y))
 
     for dd in range(nd):
-        pick = select(group * blk, gw, width, dd * width)
+        picks[dd] = select(group * blk, gw, width, dd * width)
         for q in range(n_group):
             got = jnp.dot(
-                acts_ref[:, q * group * blk:(q + 1) * group * blk], pick, preferred_element_type=F32
+                acts_ref[:, q * group * blk:(q + 1) * group * blk], picks[dd], preferred_element_type=F32
             )
             perm[dd, :, q * gw:(q + 1) * gw] = got.astype(BF16)
 
@@ -109,11 +109,59 @@
         go(rcopy(perm.at[lax.rem(d + o, nd)], act.at[m, d], aa_s.at[o], aa_r.at[o], dpeer(o)))
         for o in range(1, nd)
     ]
+    act[m, d] = perm[d]
+
+    for c in acts_sent:
+        c.wait_recv()
+
+    def along(right, src):
+        ref = act.at[src * ny + y]
+        side = 0 if right else 1
+        return rcopy(ref, ref, az_s.at[side, src], az_r.at[side, src], mpeer(z + 1 if right else z - 1, y))
+
+    def across(src, b, back):
+        ref = act.at[src * ny + (yo(-b) if back else y)]
+        return rcopy(ref, ref, ay_s.at[src, b], ay_r.at[src, b], mpeer(z, yo(b)))
+
+    def spread(src):
+        for b in range(1, ny):
+            across(src, b, False).start()
+
+    @pl.when(z < nz - 1)
+    def _():
+        along(True, z).start()
+
+    @pl.when(z > 0)
+    def _():
+        along(False, z).start()
+
+    spread(z)
+
+    def arrival(s):
+        @pl.when(z >= s)
+        def _():
+            along(True, z - s).wait_recv()
+
+            @pl.when(z < nz - 1)
+            def _():
+                along(True, z - s).start()
+
+            spread(z - s)
+
+        @pl.when(z + s < nz)
+        def _():
+            along(False, z + s).wait_recv()
+
+            @pl.when(z > 0)
+            def _():
+                along(False, z + s).start()
+
+            spread(z + s)
+
     gout_sent = [
         go(rcopy(gout_ref, gall.at[d], go_s.at[o], go_r.at[o], hpeer(o))) for o in range(1, half)
     ]
     gout_twin = [go(rcopy(gout_ref, gall.at[d], gf_s.at[0], gf_r.at[0], twin))]
-    act[m, d] = perm[d]
     gall[d] = gout_ref[...]
 
     load.wait()
@@ -127,53 +175,6 @@
                 c, slot_ref[c, r]
             ]
 
-    for c in acts_sent:
-        c.wait_recv()
-
-    def along(right, src):
-        ref = act.at[src * ny + y]
-        side = 0 if right else 1
-        return rcopy(ref, ref, az_s.at[side, src], az_r.at[side, src], mpeer(z + 1 if right else z - 1, y))
-
-    def across(src, b, back):
-        ref = act.at[src * ny + (yo(-b) if back else y)]
-        return rcopy(ref, ref, ay_s.at[src, b], ay_r.at[src, b], mpeer(z, yo(b)))
-
-    def spread(src):
-        for b in range(1, ny):
-            across(src, b, False).start()
-
-    @pl.when(z < nz - 1)
-    def _():
-        along(True, z).start()
-
-    @pl.when(z > 0)
-    def _():
-        along(False, z).start()
-
-    spread(z)
-
-    def arrival(s):
-        @pl.when(z >= s)
-        def _():
-            along(True, z - s).wait_recv()
-
-            @pl.when(z < nz - 1)
-            def _():
-                along(True, z - s).start()
-
-            spread(z - s)
-
-        @pl.when(z + s < nz)
-        def _():
-            along(False, z + s).wait_recv()
-
-            @pl.when(z > 0)
-            def _():
-                along(False, z + s).start()
-
-            spread(z + s)
-
     for o, c in enumerate(gout_sent):
         c.wait_recv()
         ref = gall.at[lax.rem(h - (o + 1) + half, half) * 2 + core]
@@ -201,12 +202,16 @@
             part.at[target(a) * ny + yo(b)], ry.at[a, b - 1], py_s.at[a, b], py_r.at[a, b], mpeer(z, yo(b))
         )
 
+    def send_y(a):
+        for b in range(1, ny):
+            go(to_y(a, b))
+
     for a in range(nz):
         for b in range(1, ny):
             partial(target(a) * ny + yo(b))
-            go(to_y(a, b))
         if a < nz - 1:
             arrival(a + 1)
+    send_y(0)
 
     @pl.loop(0, nz)
     def _(zz):
@@ -270,13 +275,11 @@
             across(src, b, True).wait_recv()
             use(src * ny + yo(-b))
 
-    sum_z(0)
-
     @pl.loop(0, nz)
     def _(zz):
         use(zz * ny + y)
 
-    sum_z(1)
+    send_y(1)
 
     @pl.loop(0, nz)
     def _(s):
@@ -290,17 +293,29 @@
         go(rcopy(hsend.at[lax.rem(d + o, nd)], hrecv.at[o - 1], hd_s.at[o], hd_r.at[o], dpeer(o)))
         for o in range(1, nd)
     ]
-    for a in range(2, nz - 1):
+
+    saves = []
+
+    def block_grad(c):
+        for k in range(slots):
+            picked[k * width:(k + 1) * width, :] = flip[rows_ref[c, k]]
+        gv[c] = jnp.dot(
+            picked[...].astype(BF16), gall[:, :, c * blk:(c + 1) * blk].reshape(nd * tok, blk),
+            preferred_element_type=F32,
+        ).reshape(slots, width, blk).astype(gv.dtype)
+        saves.append(pltpu.make_async_copy(gv.at[c], gv_hbm.at[c], gv_s.at[c]))
+        saves[-1].start()
+
+    sum_z(0)
+    for a in range(2, nz):
+        send_y(a)
+        for c in range(cols * (a - 2) // (nz - 2), cols * (a - 1) // (nz - 2)):
+            block_grad(c)
+        if a < nz - 1:
+            sum_z(a - 1)
+    for a in range(max(1, nz - 2), nz - 1):
         sum_z(a)
     sum_y(nz - 1)
-
-    for c in range(cols):
-        for k in range(slots):
-            picked[k * width:(k + 1) * width, :] = flip[rows_ref[c, k]]
-        gv_out[c] = jnp.dot(
-            picked[...].astype(BF16), gall[:, :, c * blk:(c + 1) * blk].reshape(nd * tok, blk),
-            preferred_element_type=F32,
-        ).reshape(slots, width, blk)
 
     @pl.loop(0, nd)
     def _(t):
@@ -338,13 +353,14 @@
     for q in range(n_group):
         total = jnp.zeros((tok, group * blk), F32)
         for dd in range(nd):
-            pick = select(group * blk, gw, width, dd * width)
             total += lax.dot_general(
-                garecv[dd, :, q * gw:(q + 1) * gw], pick, (((1,), (1,)), ((), ())),
+                garecv[dd, :, q * gw:(q + 1) * gw], picks[dd], (((1,), (1,)), ((), ())),
                 preferred_element_type=F32,
             )
         ga_out[:, q * group * blk:(q + 1) * group * blk] = total.astype(BF16)
 
+    for c in saves:
+        c.wait()
     for c in sends:
         c.wait_send()
     for src in range(nz):
@@ -372,6 +388,7 @@
     feat = local_blocks * width
     row_blocks = local_blocks * nm
     depth = feat * nm
+    group = min(local_blocks, blk // width)
     live = jnp.arange(slots, dtype=jnp.int32)[None, :] < block_count[:, None]
     hit = (block_rows[:, :, None] == jnp.arange(row_blocks, dtype=jnp.int32)) & live[:, :, None]
     slot_of = jnp.min(
@@ -388,16 +405,18 @@
         out_shape=(
             jax.ShapeDtypeStruct((tok, ff), BF16),
             jax.ShapeDtypeStruct((tok, local), BF16),
-            jax.ShapeDtypeStruct(values.shape, F32),
+            jax.ShapeDtypeStruct(values.shape, kind),
         ),
         in_specs=[smem] * 2 + [vmem] * 2 + [pl.BlockSpec(memory_space=pl.ANY)],
-        out_specs=(vmem,) * 3,
+        out_specs=(vmem, vmem, pl.BlockSpec(memory_space=pl.ANY)),
         scratch_shapes=[
             pltpu.VMEM((cols, slots + 1, width, blk), kind),
             pltpu.VMEM((depth, ff), kind),
             pltpu.VMEM((row_blocks, width, nd * tok), kind),
             pltpu.VMEM((nd, tok, ff), BF16),
             pltpu.VMEM((slots * width, nd * tok), kind),
+            pltpu.VMEM((nd, group * blk, group * width), BF16),
+            pltpu.VMEM(values.shape, kind),
             pltpu.VMEM((nd, tok, feat), BF16),
             pltpu.VMEM((nm, nd, tok, feat), BF16),
             pltpu.VMEM((nm, nd, tok, feat), BF16),
@@ -409,7 +428,7 @@
             pltpu.VMEM((nd, tok, feat), F32),
             pltpu.VMEM((nd, tok, feat), BF16),
             pltpu.VMEM((nd, tok, feat), BF16),
-            dma(()),
+            dma(()), dma((cols,)),
             dma((nd,)), dma((nd,)), dma((nd,)), dma((nd,)), dma((nd,)), dma((nd,)),
             dma((2, nz)), dma((2, nz)), dma((nz, ny)), dma((nz, ny)),
             dma((nz, ny)), dma((nz, ny)), dma((2, nz)), dma((2, nz)),
@@ -422,7 +441,7 @@
             flops=4 * nd * tok * depth * ff, bytes_accessed=2 ** 23, transcendentals=0
         ),
     )(block_rows, slot_of, acts, grad_out, values)
-    grad_values = jnp.where(live[:, :, None, None], grad_values, jnp.zeros((), F32))
+    grad_values = jnp.where(live[:, :, None, None], grad_values.astype(F32), jnp.zeros((), F32))
     return hidden_out, grad_acts, grad_values
 
 

time: 77.9 us -> 79.4 us (1.019)
  Pallas kernels: 69.8 us -> 71.8 us
    pallas_call x1, Pallas kernels: 69.8 us -> 71.8 us  [shards(): pl.pallas_call(functools.partial(kernel, nd, nm), out_shape=(jax.ShapeDty...]
where the time goes in v3:
time: 79.4 us; the launch traced here: 79.2 us
  Pallas kernels  71.8 us (90%)
  other arithmetic  4.44 us (6%)
  local copies, waits for them, and re-layouts  2.29 us (3%)
    pallas_call x1, Pallas kernels, shards(): pl.pallas_call(functools.partial(kernel, nd, nm), out_shape=(jax.ShapeDty...  71.8 us
    select_n x1, other arithmetic, shards(): jnp.where(live[:, :, None, None], grad_values.astype(F32), jnp.zeros((),...  3 us
    unnamed x7, local copies, waits for them, and re-layouts  2.18 us

profile of v3, /device:TPU:1, one launch (start us, length us, event | category | flops | bytes accessed | tf_op | source)
XLA Modules:
  0.0 79.2 jit_solution(12776539125328047374)
XLA Ops:
  0.6 0.7 iota_compare_fusion.1
  1.4 0.1 copy.9
  1.5 0.8 copy.8
  2.2 0.7 select_reduce_fusion.slot_ref
  3.0 71.8 %shard_map.76 = (bf16[128,896]{1,0:T(8,128)(2,1)}, bf16[128,1024]{1,0:T(8,128)(2,1)}, bf16[7,20,32,128]{3,2,1,0:T(8,128)(2,1)}) custom-call(s32[7,20]{1,0:T(8,128)} %rows_ref.1, s32[7,64]{1,0:T(8,128)} %select_reduce_fusion.slot_ref, bf16[128,1024]{1,0:T(8,128)(2,1)} %acts_ref.1, bf16[128,896]{1,0:T(8,128)(2,1)} %gout_ref.1, bf16[7,20,32,128]{3,2,1,0:T(8,128)(2,1)} %val_hbm.1), custom_call_target="tpu_custom_call" | custom-call | flops 3758096384 | bytes 8388608 | tf_op jit(solution)/shard_map/pallas_call | solution.py:403
  74.8 0.0 copy-start.1
  74.8 0.0 copy-start
  74.8 3.0 %convert_select_fusion = f32[7,20,32,128]{3,2,1,0:T(8,128)} fusion(bf16[7,20,32,128]{3,2,1,0:T(8,128)(2,1)} %get-tuple-element.8, pred[7,20]{1,0:T(8,128)(4,1)S(1)} %iota_compare_fusion.1), kind=kLoop, calls=%fused_computation | loop fusion | flops 1146880 | bytes 3440780 | tf_op jit(solution)/shard_map/jit(_where)/select_n | solution.py:444
  77.8 0.0 copy-done.1
  77.8 0.7 copy.12
  78.5 0.0 copy-done
  78.5 0.7 copy.13
Async XLA Ops:
  74.8 3.0 %copy-start.1 = (bf16[128,896]{1,0:T(8,128)(2,1)S(1)}, bf16[128,896]{1,0:T(8,128)(2,1)}, u32[]{:S(2)}) copy-start(bf16[128,896]{1,0:T(8,128)(2,1)} %get-tuple-element.12) | copy-start | bytes 688132
  74.8 3.7 %copy-start = (bf16[128,1024]{1,0:T(8,128)(2,1)S(1)}, bf16[128,1024]{1,0:T(8,128)(2,1)}, u32[]{:S(2)}) copy-start(bf16[128,1024]{1,0:T(8,128)(2,1)} %get-tuple-element.13) | copy-start | bytes 786436

commit v4 on v3

--- a/solution.py
+++ b/solution.py
@@ -111,52 +111,59 @@
     ]
     act[m, d] = perm[d]
 
-    for c in acts_sent:
-        c.wait_recv()
-
-    def along(right, src):
-        ref = act.at[src * ny + y]
+    def along(right, src, t):
+        ref = act.at[src * ny + y, t]
         side = 0 if right else 1
-        return rcopy(ref, ref, az_s.at[side, src], az_r.at[side, src], mpeer(z + 1 if right else z - 1, y))
-
-    def across(src, b, back):
-        ref = act.at[src * ny + (yo(-b) if back else y)]
-        return rcopy(ref, ref, ay_s.at[src, b], ay_r.at[src, b], mpeer(z, yo(b)))
-
-    def spread(src):
+        dev = mpeer(z + 1 if right else z - 1, y)
+        return rcopy(ref, ref, az_s.at[side, src, t], az_r.at[side, src, t], dev)
+
+    def across(src, b, back, t):
+        ref = act.at[src * ny + (yo(-b) if back else y), t]
+        return rcopy(ref, ref, ay_s.at[src, b, t], ay_r.at[src, b, t], mpeer(z, yo(b)))
+
+    def spread(src, t):
         for b in range(1, ny):
-            across(src, b, False).start()
-
-    @pl.when(z < nz - 1)
-    def _():
-        along(True, z).start()
-
-    @pl.when(z > 0)
-    def _():
-        along(False, z).start()
-
-    spread(z)
+            across(src, b, False, t).start()
+
+    for o in range(nd):
+        if o:
+            acts_sent[o - 1].wait_recv()
+        block = lax.rem(d - o + nd, nd)
+
+        @pl.when(z < nz - 1)
+        def _():
+            along(True, z, block).start()
+
+        @pl.when(z > 0)
+        def _():
+            along(False, z, block).start()
+
+        spread(z, block)
 
     def arrival(s):
-        @pl.when(z >= s)
-        def _():
-            along(True, z - s).wait_recv()
-
-            @pl.when(z < nz - 1)
-            def _():
-                along(True, z - s).start()
-
-            spread(z - s)
-
-        @pl.when(z + s < nz)
-        def _():
-            along(False, z + s).wait_recv()
-
-            @pl.when(z > 0)
-            def _():
-                along(False, z + s).start()
-
-            spread(z + s)
+        @pl.loop(0, nd)
+        def _(o):
+            t = lax.rem(d - o + nd, nd)
+
+            @pl.when(z >= s)
+            def _():
+                along(True, z - s, t).wait_recv()
+
+                @pl.when(z < nz - 1)
+                def _():
+                    along(True, z - s, t).start()
+
+                spread(z - s, t)
+
+            @pl.when(z + s < nz)
+            def _():
+                along(False, z + s, t).wait_recv()
+
+                @pl.when(z > 0)
+                def _():
+                    along(False, z + s, t).start()
+
+                spread(z + s, t)
 
     gout_sent = [
         go(rcopy(gout_ref, gall.at[d], go_s.at[o], go_r.at[o], hpeer(o))) for o in range(1, half)
@@ -197,21 +204,22 @@
         high = a + (jnp.int32(a) >= z).astype(jnp.int32)
         return z if a == nz - 1 else jnp.where(z < nz // 2, low, high)
 
-    def to_y(a, b):
+    def to_y(a, b, t):
         return rcopy(
-            part.at[target(a) * ny + yo(b)], ry.at[a, b - 1], py_s.at[a, b], py_r.at[a, b], mpeer(z, yo(b))
+            part.at[target(a) * ny + yo(b), t], ry.at[a, b - 1, t], py_s.at[a, b, t], py_r.at[a, b, t],
+            mpeer(z, yo(b)),
         )
-
-    def send_y(a):
-        for b in range(1, ny):
-            go(to_y(a, b))
 
     for a in range(nz):
         for b in range(1, ny):
             partial(target(a) * ny + yo(b))
+
+            @pl.loop(0, nd)
+            def _(t):
+                to_y(a, b, t).start()
+
         if a < nz - 1:
             arrival(a + 1)
-    send_y(0)
 
     @pl.loop(0, nz)
     def _(zz):
@@ -229,57 +237,62 @@
             local_blocks, width, nd * tok
         )
 
-    def sum_y(a):
-        mm = target(a) * ny + y
+    def to_z(zt, t):
+        right = (zt > z).astype(jnp.int32)
+        return rcopy(
+            part.at[zt * ny + y, t], rz.at[1 - right, zt, t],
+            pz_s.at[1 - right, zt, t], pz_r.at[1 - right, zt, t],
+            mpeer(z + 2 * right - 1, y),
+        )
+
+    def from_z(side, zt, t):
+        ref = rz.at[side, zt, t]
+        rcopy(ref, ref, pz_s.at[side, zt, t], pz_r.at[side, zt, t], mpeer(z, y)).wait_recv()
+
+    def over_y(a, t):
+        total = part[target(a) * ny + y, t].astype(F32)
         for b in range(1, ny):
-            to_y(a, b).wait_recv()
+            to_y(a, b, t).wait_recv()
+            total += ry[a, b - 1, t].astype(F32)
+        return total
+
+    def sum_z(a):
+        zt = target(a)
+        mm = zt * ny + y
+        side = 1 - (zt > z).astype(jnp.int32)
+        middle = jnp.where(zt > z, z > 0, z < nz - 1)
 
         @pl.loop(0, nd)
         def _(t):
-            total = part[mm, t].astype(F32)
-            for b in range(1, ny):
-                total += ry[a, b - 1, t].astype(F32)
-            part[mm, t] = total.astype(BF16)
-
-    def to_z(zt):
-        right = (zt > z).astype(jnp.int32)
-        return rcopy(
-            part.at[zt * ny + y], rz.at[1 - right, zt], pz_s.at[1 - right, zt], pz_r.at[1 - right, zt],
-            mpeer(z + 2 * right - 1, y),
-        )
-
-    def from_z(side, zt):
-        ref = rz.at[side, zt]
-        rcopy(ref, ref, pz_s.at[side, zt], pz_r.at[side, zt], mpeer(z, y)).wait_recv()
-
-    def sum_z(a):
-        zt = target(a)
-        side = 1 - (zt > z).astype(jnp.int32)
-        sum_y(a)
-
-        @pl.when(jnp.where(zt > z, z > 0, z < nz - 1))
-        def _():
-            from_z(side, zt)
-
-            @pl.loop(0, nd)
-            def _(t):
-                part[zt * ny + y, t] = (
-                    part[zt * ny + y, t].astype(F32) + rz[side, zt, t].astype(F32)
-                ).astype(BF16)
-
-        to_z(zt).start()
+            total = over_y(a, t)
+
+            @pl.when(middle)
+            def _():
+                from_z(side, zt, t)
+                part[mm, t] = (total + rz[side, zt, t].astype(F32)).astype(BF16)
+
+            @pl.when(jnp.logical_not(middle))
+            def _():
+                part[mm, t] = total.astype(BF16)
+
+            to_z(zt, t).start()
 
     def use_far(s):
         src = lax.rem(z + s, nz)
         for b in range(1, ny):
-            across(src, b, True).wait_recv()
+            @pl.loop(0, nd)
+            def _(t):
+                across(src, b, True, t).wait_recv()
+
             use(src * ny + yo(-b))
+
+    sum_z(0)
 
     @pl.loop(0, nz)
     def _(zz):
         use(zz * ny + y)
 
-    send_y(1)
+    sum_z(1)
 
     @pl.loop(0, nz)
     def _(s):
@@ -306,40 +319,32 @@
         saves.append(pltpu.make_async_copy(gv.at[c], gv_hbm.at[c], gv_s.at[c]))
         saves[-1].start()
 
-    sum_z(0)
-    for a in range(2, nz):
-        send_y(a)
-        for c in range(cols * (a - 2) // (nz - 2), cols * (a - 1) // (nz - 2)):
-            block_grad(c)
-        if a < nz - 1:
-            sum_z(a - 1)
-    for a in range(max(1, nz - 2), nz - 1):
+    for c in range(cols // 2):
+        block_grad(c)
+    for a in range(2, nz - 1):
         sum_z(a)
-    sum_y(nz - 1)
+
+    def to_dp(t):
+        return rcopy(gasend.at[t], garecv.at[d], ga_s.at[t], ga_r.at[d], (t, m))
 
     @pl.loop(0, nd)
-    def _(t):
-        tot[t] = part[m, t].astype(F32)
-
-    for side in range(2):
-        @pl.when(z > 0 if side == 0 else z < nz - 1)
+    def _(o):
+        t = lax.rem(d + 1 + o, nd)
+        tot[...] = over_y(nz - 1, t)
+        for side in range(2):
+            @pl.when(z > 0 if side == 0 else z < nz - 1)
+            def _():
+                from_z(side, z, t)
+                tot[...] += rz[side, z, t].astype(F32)
+        gasend[t] = tot[...].astype(BF16)
+
+        @pl.when(t != d)
         def _():
-            from_z(side, z)
-
-            @pl.loop(0, nd)
-            def _(t):
-                tot[t] += rz[side, z, t].astype(F32)
-
-    @pl.loop(0, nd)
-    def _(t):
-        gasend[t] = tot[t].astype(BF16)
+            to_dp(t).start()
 
     garecv[d] = gasend[d]
-
-    ga_sent = [
-        go(rcopy(gasend.at[lax.rem(d + o, nd)], garecv.at[d], ga_s.at[o], ga_r.at[o], dpeer(o)))
-        for o in range(1, nd)
-    ]
+    for c in range(cols // 2, cols):
+        block_grad(c)
 
     for c in hid_sent:
         c.wait_recv()
@@ -348,8 +353,9 @@
         total += hrecv[o - 1].astype(F32)
     hid_out[...] = total.astype(BF16)
 
-    for c in ga_sent:
-        c.wait_recv()
+    for o in range(1, nd):
+        src = lax.rem(d + o, nd)
+        rcopy(gasend.at[src], garecv.at[src], ga_s.at[src], ga_r.at[src], (src, m)).wait_recv()
     for q in range(n_group):
         total = jnp.zeros((tok, group * blk), F32)
         for dd in range(nd):
@@ -363,19 +369,28 @@
         c.wait()
     for c in sends:
         c.wait_send()
-    for src in range(nz):
-        for b in range(1, ny):
-            across(src, b, False).wait_send()
-
-        @pl.when((z < nz - 1) & (z >= src))
+
+    @pl.loop(0, nd)
+    def _(t):
+        for src in range(nz):
+            for b in range(1, ny):
+                across(src, b, False, t).wait_send()
+                to_y(src, b, t).wait_send()
+
+            @pl.when((z < nz - 1) & (z >= src))
+            def _():
+                along(True, src, t).wait_send()
+
+            @pl.when((z > 0) & (z <= src))
+            def _():
+                along(False, src, t).wait_send()
+
+        for a in range(nz - 1):
+            to_z(target(a), t).wait_send()
+
+        @pl.when(t != d)
         def _():
-            along(True, src).wait_send()
-
-        @pl.when((z > 0) & (z <= src))
-        def _():
-            along(False, src).wait_send()
-    for a in range(nz - 1):
-        to_z(target(a)).wait_send()
+            to_dp(t).wait_send()
 
 
 def shards(nd, nm, acts, grad_out, values, block_rows, block_count):
@@ -425,13 +440,13 @@
             pltpu.VMEM((nd, tok, ff), F32),
             pltpu.VMEM((nd, tok, ff), BF16),
             pltpu.VMEM((nd - 1, tok, ff), BF16),
-            pltpu.VMEM((nd, tok, feat), F32),
+            pltpu.VMEM((tok, feat), F32),
             pltpu.VMEM((nd, tok, feat), BF16),
             pltpu.VMEM((nd, tok, feat), BF16),
             dma(()), dma((cols,)),
             dma((nd,)), dma((nd,)), dma((nd,)), dma((nd,)), dma((nd,)), dma((nd,)),
-            dma((2, nz)), dma((2, nz)), dma((nz, ny)), dma((nz, ny)),
-            dma((nz, ny)), dma((nz, ny)), dma((2, nz)), dma((2, nz)),
+            dma((2, nz, nd)), dma((2, nz, nd)), dma((nz, ny, nd)), dma((nz, ny, nd)),
+            dma((nz, ny, nd)), dma((nz, ny, nd)), dma((2, nz, nd)), dma((2, nz, nd)),
             dma((nd,)), dma((nd,)), dma((nd,)), dma((nd,)),
         ],
         compiler_params=pltpu.CompilerParams(

time: 79.4 us -> 80.1 us (level)
  no operation moved by 1% of the time
where the time goes in v4:
time: 80.1 us; the launch traced here: 79.8 us
  Pallas kernels  72.4 us (90%)
  other arithmetic  4.44 us (6%)
  local copies, waits for them, and re-layouts  2.29 us (3%)
    pallas_call x1, Pallas kernels, shards(): pl.pallas_call(functools.partial(kernel, nd, nm), out_shape=(jax.ShapeDty...  72.4 us
    select_n x1, other arithmetic, shards(): jnp.where(live[:, :, None, None], grad_values.astype(F32), jnp.zeros((),...  3 us
    unnamed x7, local copies, waits for them, and re-layouts  2.18 us

profile of v4, /device:TPU:1, one launch (start us, length us, event | category | flops | bytes accessed | tf_op | source)
XLA Modules:
  0.0 79.8 jit_solution(3646691011596337532)
XLA Ops:
  0.6 0.7 iota_compare_fusion.1
  1.4 0.1 copy.9
  1.5 0.8 copy.8
  2.2 0.7 select_reduce_fusion.slot_ref
  3.0 72.4 %shard_map.76 = (bf16[128,896]{1,0:T(8,128)(2,1)}, bf16[128,1024]{1,0:T(8,128)(2,1)}, bf16[7,20,32,128]{3,2,1,0:T(8,128)(2,1)}) custom-call(s32[7,20]{1,0:T(8,128)} %rows_ref.1, s32[7,64]{1,0:T(8,128)} %select_reduce_fusion.slot_ref, bf16[128,1024]{1,0:T(8,128)(2,1)} %acts_ref.1, bf16[128,896]{1,0:T(8,128)(2,1)} %gout_ref.1, bf16[7,20,32,128]{3,2,1,0:T(8,128)(2,1)} %val_hbm.1), custom_call_target="tpu_custom_call" | custom-call | flops 3758096384 | bytes 8388608 | tf_op jit(solution)/shard_map/pallas_call | solution.py:418
  75.4 0.0 copy-start.1
  75.4 0.0 copy-start
  75.4 3.0 %convert_select_fusion = f32[7,20,32,128]{3,2,1,0:T(8,128)} fusion(bf16[7,20,32,128]{3,2,1,0:T(8,128)(2,1)} %get-tuple-element.8, pred[7,20]{1,0:T(8,128)(4,1)S(1)} %iota_compare_fusion.1), kind=kLoop, calls=%fused_computation | loop fusion | flops 1146880 | bytes 3440780 | tf_op jit(solution)/shard_map/jit(_where)/select_n | solution.py:459
  78.4 0.0 copy-done.1
  78.4 0.7 copy.12
  79.1 0.0 copy-done
  79.1 0.7 copy.13
Async XLA Ops:
  75.4 3.0 %copy-start.1 = (bf16[128,896]{1,0:T(8,128)(2,1)S(1)}, bf16[128,896]{1,0:T(8,128)(2,1)}, u32[]{:S(2)}) copy-start(bf16[128,896]{1,0:T(8,128)(2,1)} %get-tuple-element.12) | copy-start | bytes 688132
  75.4 3.7 %copy-start = (bf16[128,1024]{1,0:T(8,128)(2,1)S(1)}, bf16[128,1024]{1,0:T(8,128)(2,1)}, u32[]{:S(2)}) copy-start(bf16[128,1024]{1,0:T(8,128)(2,1)} %get-tuple-element.13) | copy-start | bytes 786436

commit v5 on v2

--- a/solution.py
+++ b/solution.py
@@ -22,11 +22,11 @@
 
 def kernel(
     nd, nm,
-    rows_ref, slot_ref, acts_ref, gout_ref, val_hbm,
-    hid_out, ga_out, gv_out,
-    val, w, flip, gall, picked,
+    rows_ref, count_ref, acts_ref, gout_ref, val_hbm,
+    hid_out, ga_out, gv_hbm,
+    slot_v, slot_ref, val, w, flip, gall, picked, picks, gv,
     perm, act, part, ry, rz, hid, hsend, hrecv, tot, gasend, garecv,
-    val_s, aa_s, aa_r, go_s, go_r, gf_s, gf_r, az_s, az_r, ay_s, ay_r,
+    val_s, slot_s, gv_s, aa_s, aa_r, go_s, go_r, gf_s, gf_r, az_s, az_r, ay_s, ay_r,
     py_s, py_r, pz_s, pz_r, hd_s, hd_r, ga_s, ga_r,
 ):
     nz = N_Z
@@ -88,12 +88,23 @@
         greet(mpeer(z + 1, y))
 
     for dd in range(nd):
-        pick = select(group * blk, gw, width, dd * width)
+        picks[dd] = select(group * blk, gw, width, dd * width)
         for q in range(n_group):
             got = jnp.dot(
-                acts_ref[:, q * group * blk:(q + 1) * group * blk], pick, preferred_element_type=F32
+                acts_ref[:, q * group * blk:(q + 1) * group * blk], picks[dd], preferred_element_type=F32
             )
             perm[dd, :, q * gw:(q + 1) * gw] = got.astype(BF16)
+
+    lane = lax.broadcasted_iota(jnp.int32, (1, slot_v.shape[1]), 1)
+    slot_v[...] = jnp.zeros_like(slot_v)
+    for c in range(cols):
+        found = jnp.full(lane.shape, slots, jnp.int32)
+        for k in range(slots):
+            row = jnp.where(k < count_ref[c], rows_ref[c, k], -1)
+            found = jnp.where(lane == row, k, found)
+        slot_v[c:c + 1, :] = found
+    to_scalar = pltpu.make_async_copy(slot_v, slot_ref, slot_s)
+    to_scalar.start()
 
     ends = (z == 0).astype(jnp.int32) + (z == nz - 1).astype(jnp.int32)
     pl.semaphore_wait(barrier, len(peers) + 2 - ends)
@@ -117,6 +128,7 @@
     gall[d] = gout_ref[...]
 
     load.wait()
+    to_scalar.wait()
     for c in range(cols):
         val[c, slots] = jnp.zeros((width, blk), val.dtype)
 
@@ -290,17 +302,25 @@
         go(rcopy(hsend.at[lax.rem(d + o, nd)], hrecv.at[o - 1], hd_s.at[o], hd_r.at[o], dpeer(o)))
         for o in range(1, nd)
     ]
-    for a in range(2, nz - 1):
-        sum_z(a)
-    sum_y(nz - 1)
-
-    for c in range(cols):
+    saves = []
+    order = lax.broadcasted_iota(jnp.int32, (slots, width, blk), 0)
+
+    def block_grad(c):
         for k in range(slots):
             picked[k * width:(k + 1) * width, :] = flip[rows_ref[c, k]]
-        gv_out[c] = jnp.dot(
+        got = jnp.dot(
             picked[...].astype(BF16), gall[:, :, c * blk:(c + 1) * blk].reshape(nd * tok, blk),
             preferred_element_type=F32,
         ).reshape(slots, width, blk)
+        gv[c] = jnp.where(order < count_ref[c], got, 0.0).astype(gv.dtype)
+        saves.append(pltpu.make_async_copy(gv.at[c], gv_hbm.at[c], gv_s.at[c]))
+        saves[-1].start()
+
+    for a in range(2, nz - 1):
+        sum_z(a)
+    for c in range(cols // 2):
+        block_grad(c)
+    sum_y(nz - 1)
 
     @pl.loop(0, nd)
     def _(t):
@@ -325,6 +345,9 @@
         go(rcopy(gasend.at[lax.rem(d + o, nd)], garecv.at[d], ga_s.at[o], ga_r.at[o], dpeer(o)))
         for o in range(1, nd)
     ]
+
+    for c in range(cols // 2, cols):
+        block_grad(c)
 
     for c in hid_sent:
         c.wait_recv()
@@ -338,13 +361,14 @@
     for q in range(n_group):
         total = jnp.zeros((tok, group * blk), F32)
         for dd in range(nd):
-            pick = select(group * blk, gw, width, dd * width)
             total += lax.dot_general(
-                garecv[dd, :, q * gw:(q + 1) * gw], pick, (((1,), (1,)), ((), ())),
+                garecv[dd, :, q * gw:(q + 1) * gw], picks[dd], (((1,), (1,)), ((), ())),
                 preferred_element_type=F32,
             )
         ga_out[:, q * group * blk:(q + 1) * group * blk] = total.astype(BF16)
 
+    for c in saves:
+        c.wait()
     for c in sends:
         c.wait_send()
     for src in range(nz):
@@ -372,14 +396,12 @@
     feat = local_blocks * width
     row_blocks = local_blocks * nm
     depth = feat * nm
-    live = jnp.arange(slots, dtype=jnp.int32)[None, :] < block_count[:, None]
-    hit = (block_rows[:, :, None] == jnp.arange(row_blocks, dtype=jnp.int32)) & live[:, :, None]
-    slot_of = jnp.min(
-        jnp.where(hit, jnp.arange(slots, dtype=jnp.int32)[None, :, None], slots), axis=1
-    )
+    group = min(local_blocks, blk // width)
     if width % 16:
         values = values.astype(F32)
     kind = values.dtype
+    slot_rows = -(-cols // 8) * 8
+    slot_lanes = -(-row_blocks // 128) * 128
     dma = pltpu.SemaphoreType.DMA
     vmem = pl.BlockSpec(memory_space=pltpu.VMEM)
     smem = pl.BlockSpec(memory_space=pltpu.SMEM)
@@ -388,16 +410,20 @@
         out_shape=(
             jax.ShapeDtypeStruct((tok, ff), BF16),
             jax.ShapeDtypeStruct((tok, local), BF16),
-            jax.ShapeDtypeStruct(values.shape, F32),
+            jax.ShapeDtypeStruct(values.shape, kind),
         ),
         in_specs=[smem] * 2 + [vmem] * 2 + [pl.BlockSpec(memory_space=pl.ANY)],
-        out_specs=(vmem,) * 3,
+        out_specs=(vmem, vmem, pl.BlockSpec(memory_space=pl.ANY)),
         scratch_shapes=[
+            pltpu.VMEM((slot_rows, slot_lanes), jnp.int32),
+            pltpu.SMEM((slot_rows, slot_lanes), jnp.int32),
             pltpu.VMEM((cols, slots + 1, width, blk), kind),
             pltpu.VMEM((depth, ff), kind),
             pltpu.VMEM((row_blocks, width, nd * tok), kind),
             pltpu.VMEM((nd, tok, ff), BF16),
             pltpu.VMEM((slots * width, nd * tok), kind),
+            pltpu.VMEM((nd, group * blk, group * width), BF16),
+            pltpu.VMEM(values.shape, kind),
             pltpu.VMEM((nd, tok, feat), BF16),
             pltpu.VMEM((nm, nd, tok, feat), BF16),
             pltpu.VMEM((nm, nd, tok, feat), BF16),
@@ -409,7 +435,7 @@
             pltpu.VMEM((nd, tok, feat), F32),
             pltpu.VMEM((nd, tok, feat), BF16),
             pltpu.VMEM((nd, tok, feat), BF16),
-            dma(()),
+            dma(()), dma(()), dma((cols,)),
             dma((nd,)), dma((nd,)), dma((nd,)), dma((nd,)), dma((nd,)), dma((nd,)),
             dma((2, nz)), dma((2, nz)), dma((nz, ny)), dma((nz, ny)),
             dma((nz, ny)), dma((nz, ny)), dma((2, nz)), dma((2, nz)),
@@ -421,9 +447,8 @@
         cost_estimate=pl.CostEstimate(
             flops=4 * nd * tok * depth * ff, bytes_accessed=2 ** 23, transcendentals=0
         ),
-    )(block_rows, slot_of, acts, grad_out, values)
-    grad_values = jnp.where(live[:, :, None, None], grad_values, jnp.zeros((), F32))
-    return hidden_out, grad_acts, grad_values
+    )(block_rows, block_count, acts, grad_out, values)
+    return hidden_out, grad_acts, grad_values.astype(F32)
 
 
 def solution(mesh):

time: 77.9 us -> 74.5 us (0.956)
  other arithmetic: 4.76 us -> 3.01 us
  local copies, waits for them, and re-layouts: 2.29 us -> 1.4 us
    select_n x1 -> x0, other arithmetic: 3.32 us -> none  [shards(): jnp.where(live[:, :, None, None], grad_values, jnp.zeros((), F32))]
    convert_element_type x0 -> x1, other arithmetic: none -> 3.01 us  [shards(): return (hidden_out, grad_acts, grad_values.astype(F32))]
    unnamed x7 -> x6, local copies, waits for them, and re-layouts: 2.18 us -> 1.4 us
where the time goes in v5:
time: 74.5 us; the launch traced here: 74.2 us
  Pallas kernels  69.1 us (93%)
  other arithmetic  3.01 us (4%)
  local copies, waits for them, and re-layouts  1.4 us (2%)
    pallas_call x1, Pallas kernels, shards(): pl.pallas_call(functools.partial(kernel, nd, nm), out_shape=(jax.ShapeDty...  69.1 us
    convert_element_type x1, other arithmetic, shards(): return (hidden_out, grad_acts, grad_values.astype(F32))  3.01 us

profile of v5, /device:TPU:1, one launch (start us, length us, event | category | flops | bytes accessed | tf_op | source)
XLA Modules:
  0.0 74.2 jit_solution(1444647404148421738)
XLA Ops:
  0.6 69.1 %shard_map.76 = (bf16[128,896]{1,0:T(8,128)(2,1)}, bf16[128,1024]{1,0:T(8,128)(2,1)}, bf16[7,20,32,128]{3,2,1,0:T(8,128)(2,1)}) custom-call(s32[7,20]{1,0:T(8,128)} %rows_ref.1, s32[7]{0:T(128)} %count_ref.1, bf16[128,1024]{1,0:T(8,128)(2,1)} %acts_ref.1, bf16[128,896]{1,0:T(8,128)(2,1)} %gout_ref.1, bf16[7,20,32,128]{3,2,1,0:T(8,128)(2,1)} %val_hbm.1), custom_call_target="tpu_custom_call" | custom-call | flops 3758096384 | bytes 8388608 | tf_op jit(solution)/shard_map/pallas_call | solution.py:408
  69.7 0.0 copy-start.1
  69.7 0.0 copy-start
  69.8 3.0 %convert_element_type.3 = f32[7,20,32,128]{3,2,1,0:T(8,128)} convert(bf16[7,20,32,128]{3,2,1,0:T(8,128)(2,1)} %get-tuple-element.8) | non-fusion elementwise | flops 573440 | bytes 3440640 | tf_op jit(solution)/shard_map/convert_element_type | solution.py:451
  72.8 0.0 copy-done.1
  72.8 0.7 copy.10
  73.5 0.0 copy-done
  73.5 0.7 copy.11
Async XLA Ops:
  69.7 3.0 %copy-start.1 = (bf16[128,896]{1,0:T(8,128)(2,1)S(1)}, bf16[128,896]{1,0:T(8,128)(2,1)}, u32[]{:S(2)}) copy-start(bf16[128,896]{1,0:T(8,128)(2,1)} %get-tuple-element.12) | copy-start | bytes 688132
  69.7 3.7 %copy-start = (bf16[128,1024]{1,0:T(8,128)(2,1)S(1)}, bf16[128,1024]{1,0:T(8,128)(2,1)}, u32[]{:S(2)}) copy-start(bf16[128,1024]{1,0:T(8,128)(2,1)} %get-tuple-element.13) | copy-start | bytes 786436

commit v6 on v5

--- a/solution.py
+++ b/solution.py
@@ -127,6 +127,32 @@
     act[m, d] = perm[d]
     gall[d] = gout_ref[...]
 
+    for c in acts_sent:
+        c.wait_recv()
+
+    def along(right, src):
+        ref = act.at[src * ny + y]
+        side = 0 if right else 1
+        return rcopy(ref, ref, az_s.at[side, src], az_r.at[side, src], mpeer(z + 1 if right else z - 1, y))
+
+    def across(src, b, back):
+        ref = act.at[src * ny + (yo(-b) if back else y)]
+        return rcopy(ref, ref, ay_s.at[src, b], ay_r.at[src, b], mpeer(z, yo(b)))
+
+    def spread(src):
+        for b in range(1, ny):
+            across(src, b, False).start()
+
+    @pl.when(z < nz - 1)
+    def _():
+        along(True, z).start()
+
+    @pl.when(z > 0)
+    def _():
+        along(False, z).start()
+
+    spread(z)
+
     load.wait()
     to_scalar.wait()
     for c in range(cols):
@@ -138,32 +164,6 @@
             w[pl.ds(pl.multiple_of(r * width, width), width), c * blk:(c + 1) * blk] = val[
                 c, slot_ref[c, r]
             ]
-
-    for c in acts_sent:
-        c.wait_recv()
-
-    def along(right, src):
-        ref = act.at[src * ny + y]
-        side = 0 if right else 1
-        return rcopy(ref, ref, az_s.at[side, src], az_r.at[side, src], mpeer(z + 1 if right else z - 1, y))
-
-    def across(src, b, back):
-        ref = act.at[src * ny + (yo(-b) if back else y)]
-        return rcopy(ref, ref, ay_s.at[src, b], ay_r.at[src, b], mpeer(z, yo(b)))
-
-    def spread(src):
-        for b in range(1, ny):
-            across(src, b, False).start()
-
-    @pl.when(z < nz - 1)
-    def _():
-        along(True, z).start()
-
-    @pl.when(z > 0)
-    def _():
-        along(False, z).start()
-
-    spread(z)
 
     def arrival(s):
         @pl.when(z >= s)

time: 74.5 us -> 74.5 us (level)
  no operation moved by 1% of the time
where the time goes in v6:
time: 74.5 us; the launch traced here: 74.2 us
  Pallas kernels  69.1 us (93%)
  other arithmetic  3.01 us (4%)
  local copies, waits for them, and re-layouts  1.4 us (2%)
    pallas_call x1, Pallas kernels, shards(): pl.pallas_call(functools.partial(kernel, nd, nm), out_shape=(jax.ShapeDty...  69.1 us
    convert_element_type x1, other arithmetic, shards(): return (hidden_out, grad_acts, grad_values.astype(F32))  3.01 us

profile of v6, /device:TPU:1, one launch (start us, length us, event | category | flops | bytes accessed | tf_op | source)
XLA Modules:
  0.0 74.2 jit_solution(10532230396865155082)
XLA Ops:
  0.6 69.1 %shard_map.76 = (bf16[128,896]{1,0:T(8,128)(2,1)}, bf16[128,1024]{1,0:T(8,128)(2,1)}, bf16[7,20,32,128]{3,2,1,0:T(8,128)(2,1)}) custom-call(s32[7,20]{1,0:T(8,128)} %rows_ref.1, s32[7]{0:T(128)} %count_ref.1, bf16[128,1024]{1,0:T(8,128)(2,1)} %acts_ref.1, bf16[128,896]{1,0:T(8,128)(2,1)} %gout_ref.1, bf16[7,20,32,128]{3,2,1,0:T(8,128)(2,1)} %val_hbm.1), custom_call_target="tpu_custom_call" | custom-call | flops 3758096384 | bytes 8388608 | tf_op jit(solution)/shard_map/pallas_call | solution.py:408
  69.7 0.0 copy-start.1
  69.7 0.0 copy-start
  69.8 3.0 %convert_element_type.3 = f32[7,20,32,128]{3,2,1,0:T(8,128)} convert(bf16[7,20,32,128]{3,2,1,0:T(8,128)(2,1)} %get-tuple-element.8) | non-fusion elementwise | flops 573440 | bytes 3440640 | tf_op jit(solution)/shard_map/convert_element_type | solution.py:451
  72.8 0.0 copy-done.1
  72.8 0.7 copy.10
  73.5 0.0 copy-done
  73.5 0.7 copy.11
Async XLA Ops:
  69.7 3.0 %copy-start.1 = (bf16[128,896]{1,0:T(8,128)(2,1)S(1)}, bf16[128,896]{1,0:T(8,128)(2,1)}, u32[]{:S(2)}) copy-start(bf16[128,896]{1,0:T(8,128)(2,1)} %get-tuple-element.12) | copy-start | bytes 688132
  69.7 3.7 %copy-start = (bf16[128,1024]{1,0:T(8,128)(2,1)S(1)}, bf16[128,1024]{1,0:T(8,128)(2,1)}, u32[]{:S(2)}) copy-start(bf16[128,1024]{1,0:T(8,128)(2,1)} %get-tuple-element.13) | copy-start | bytes 786436
